TPU v7x, 512 devices: a whole 4x8x8 slice. The times are simulated.
512 devices in a mesh: dp: 64 (over z_hi, y, x), tensor: 8 (over z_lo, core).
Axes of the slice: x: 4, y: 8, z: 8 (z_hi: 2, z_lo: 4; z = z_hi * 4 + z_lo), core: 2. Of those that a mesh axis runs over, the one named last changes fastest.
Arguments:
- inputs: bfloat16 [131072, 1408], P('dp'), may hold values from -6 to 6
- up_weight: bfloat16 [1408, 6144], P(None, 'tensor'), may hold values from -0.15625 to 0.15625
- out_grad: bfloat16 [131072, 1408], P('dp', 'tensor'), may hold values from -6 to 6
- proj_in: bfloat16 [6144, 64], P('tensor'), may hold values from -0.078125 to 0.078125
- proj_out: bfloat16 [1408, 64], P('tensor'), may hold values from -0.15625 to 0.15625
- queries: bfloat16 [1024, 4096], P('dp', 'tensor'), may hold values from -0.009765625 to 0.009765625
- lengths: int32 [64, 8], P('dp'), may hold values from 1 to 3, 16 in all within a row
Outputs:
- scores: float32 [512, 1024], P('dp', 'tensor')
Inputs may be any that keep to these rules, and one draw needn't show every extreme that they name: Each row of lengths sums to 16, and some scene of each row has 3 blocks.
All inputs are finite; a program needn't handle non-finite values.
Results may differ from a plain program's by a relative error of at most 0.014.
Values may be sent and summed in bfloat16 or wider, within the bound.
No kernel may reach another device: no remote copies, remote signals or barrier semaphores. Data moves between devices by JAX's collectives and lax.ppermute only.
A program may use at most 64 MiB of HBM per device.

v0:
```python
import jax
import jax.numpy as jnp
from jax import lax
from jax.sharding import PartitionSpec as P


def scene_member(lengths, count, block_size):
    ends = block_size * jnp.cumsum(lengths[0])
    starts = ends - block_size * lengths[0]
    position = jnp.arange(count, dtype=jnp.int32)
    return ((position[None, :] >= starts[:, None]) & (position[None, :] < ends[:, None])).astype(
        jnp.float32
    )


def local(inputs, up_weight, out_grad, proj_in, proj_out, queries, lengths):
    tok_rows = inputs.shape[0]
    scene_count = lengths.shape[1]
    rank_size = proj_in.shape[1]
    feat_local = queries.shape[1]
    tensor_index = lax.axis_index("tensor")
    hidden = jax.nn.gelu(
        jnp.dot(inputs, up_weight, preferred_element_type=jnp.float32), approximate=False
    ).astype(jnp.bfloat16)
    in_part = jnp.dot(hidden, proj_in, preferred_element_type=jnp.float32)
    out_part = jnp.dot(out_grad, proj_out, preferred_element_type=jnp.float32)
    in_proj, out_proj = lax.psum((in_part, out_part), "tensor")
    member = scene_member(lengths, tok_rows, 128)
    feats = jnp.einsum("st,ti,tj->sij", member, out_proj, in_proj).reshape(
        scene_count, rank_size * rank_size
    )
    own_feats = lax.dynamic_slice_in_dim(feats, tensor_index * feat_local, feat_local, 1)
    feat_bf = own_feats.astype(jnp.bfloat16)
    partial_scores = lax.dot_general(
        feat_bf,
        lax.all_gather(queries, "dp", axis=0, tiled=True),
        (((1,), (1,)), ((), ())),
        preferred_element_type=jnp.float32,
    )
    return lax.psum_scatter(partial_scores, "tensor", scatter_dimension=1, tiled=True)


def solution(mesh):
    return jax.shard_map(
        local,
        mesh=mesh,
        in_specs=(
            P("dp", None),
            P(None, "tensor"),
            P("dp", "tensor"),
            P("tensor", None),
            P("tensor", None),
            P("dp", "tensor"),
            P("dp", None),
        ),
        out_specs=P("dp", "tensor"),
        check_vma=False,
    )
```

profile of v0, /device:TPU:1, one launch (start us, length us, event | category | flops | bytes accessed | tf_op | source)
XLA Modules:
  0.0 190.8 jit_solution(3816637453474586247)
XLA Ops:
  7.4 0.0 copy-start
  7.4 0.0 all-reduce.3.cloned.1.call-start
  7.4 2.3 %fusion.55 = f32[2048,64]{0,1:T(8,128)} fusion(bf16[176,64]{0,1:T(8,128)(2,1)} %param.11, bf16[2048,176]{0,1:T(8,128)(2,1)} %param.9), kind=kOutput, calls=%fused_computation.66 | convolution fusion | flops 46137344 | bytes 1267712 | tf_op jit(solution)/shard_map/dot_general | solution.py:26
  9.7 0.0 all-reduce.3.cloned.1.call-update
  9.7 0.0 all-gather.2.cloned.1.call-start
  9.8 0.5 all-gather.2.cloned.1.call-update
  10.3 0.0 copy-start.1
  10.3 0.0 reduce-scatter.2.cloned.1.call-start
  10.4 0.0 copy-done
  10.4 19.5 %fusion.12 = f32[2048,64]{0,1:T(8,128)S(1)} fusion(bf16[768,64]{0,1:T(8,128)(2,1)} %param.10, bf16[2048,1408]{1,0:T(8,128)(2,1)} %param.7, bf16[1408,768]{1,0:T(8,128)(2,1)S(1)} %copy-done), kind=kOutput, calls=%fused_computation.21 | convolution fusion | flops 4732747776 | bytes 8552448 | tf_op jit(solution)/shard_map/dot_general | solution.py:25
  29.9 0.0 copy-done.1
  29.9 0.2 reduce-window.7
  30.1 0.1 convert_bitcast_fusion
  30.2 36.4 %all-reduce.4 = bf16[2048,64]{0,1:T(8,128)(2,1)S(1)} all-reduce(f32[2048,64]{0,1:T(8,128)S(1)} %fusion.12), channel_id=1, replica_groups=mesh['dp'=64,'tensor'=8] {'tensor'}, use_global_device_ids=true, to_apply=%region_2.0 | all-reduce | flops 131072 | bytes 786432 | tf_op jit(solution)/shard_map/psum | solution.py:27
  66.6 26.5 %all-reduce.3.cloned.1.call-done = f32[2048,64]{0,1:T(8,128)} async-done(((f32[2048,64]{0,1:T(8,128)}), f32[2048,64]{0,1:T(8,128)}) %all-reduce.3.cloned.1.call-update) | async-done | bytes 524304 | tf_op jit(solution)/shard_map/psum | solution.py:27
  93.1 1.7 fusion.16
  94.9 0.2 reshape.33
  95.1 51.7 %all-gather.2.cloned.1.call-done = bf16[1024,512]{1,0:T(8,128)(2,1)} async-done(((bf16[16,512]{1,0:T(8,128)(2,1)}), bf16[1024,512]{1,0:T(8,128)(2,1)}) %all-gather.2.cloned.1.call-update) | async-done | bytes 1048592 | tf_op jit(solution)/shard_map/all_gather | solution.py:36
  146.7 2.2 %fusion.21 = f32[8,1024]{1,0:T(8,128)} fusion(bf16[1024,512]{1,0:T(8,128)(2,1)} %all-gather.2.cloned.1.call-done, bf16[8,4096]{1,0:T(8,128)(2,1)S(1)} %reshape.33, s32[]{:T(128)S(6)} %select_n.3), kind=kOutput, calls=%fused_computation.31 | convolution fusion | flops 8388608 | bytes 1089540 | tf_op jit(solution)/shard_map/dot_general | solution.py:34
  148.9 0.0 reduce-scatter.2.cloned.1.call-update
  149.0 34.4 %reduce-scatter.2.cloned.1.call-done = f32[8,128]{1,0:T(8,128)} async-done(((f32[8,1024]{1,0:T(8,128)}), f32[8,128]{1,0:T(8,128)}) %reduce-scatter.2.cloned.1.call-update) | async-done | bytes 4112 | tf_op jit(solution)/shard_map/reduce_scatter | solution.py:40
  (3 shorter events, 0.0 us)
Async XLA Ops:
  7.4 3.0 %copy-start = (bf16[1408,768]{1,0:T(8,128)(2,1)S(1)}, bf16[1408,768]{1,0:T(8,128)(2,1)}, u32[]{:S(2)}) copy-start(bf16[1408,768]{1,0:T(8,128)(2,1)} %param.8) | copy-start | bytes 6488068
  7.4 85.7 %all-reduce.3.cloned.1.call-start = ((), (), s32[]{:S(2)}) async-start(), calls=%async_computation.1 | async-start | bytes 1048576 | tf_op jit(solution)/shard_map/psum | solution.py:27
  9.7 137.0 %all-gather.2.cloned.1.call-start = ((), (), s32[]{:S(2)}) async-start(), calls=%async_computation.2 | async-start | bytes 1064960 | tf_op jit(solution)/shard_map/all_gather | solution.py:36
  10.3 19.6 %copy-start.1 = (s32[1,8]{1,0:T(1,128)S(1)}, s32[1,8]{1,0:T(1,128)}, u32[]{:S(2)}) copy-start(s32[1,8]{1,0:T(1,128)} %param.13) | copy-start | bytes 100
  10.3 173.0 %reduce-scatter.2.cloned.1.call-start = ((), (), s32[]{:S(2)}) async-start(), calls=%async_computation.3 | async-start | bytes 36864 | tf_op jit(solution)/shard_map/reduce_scatter | solution.py:40
Sparse Core Ops, SparseCore 0:
  11.1 81.9 all-reduce.2
  149.1 34.2 reduce-scatter.1
Sparse Core Ops, SparseCore 1:
  15.5 131.1 all-gather.1
where the time goes:
time: 193 us; the launch traced here: 191 us
  waiting for transfers between devices  113 us (59%)
  blocking collectives  36.4 us (19%)
  matrix products  25.8 us (13%)
  between operations  14.9 us (8%)
    all_gather x1, waiting for transfers between devices, local(): lax.all_gather(queries, 'dp', axis=0, tiled=True)  51.7 us
    psum x1, blocking collectives, local(): in_proj, out_proj = lax.psum((in_part, out_part), 'tensor')  36.4 us
    reduce_scatter x1, waiting for transfers between devices, local(): lax.psum_scatter(partial_scores, 'tensor', scatter_dimension=1, tiled=True)  34.4 us
    psum x1, waiting for transfers between devices, local(): in_proj, out_proj = lax.psum((in_part, out_part), 'tensor')  26.5 us
    dot_general x1, matrix products, local(): in_part = jnp.dot(hidden, proj_in, preferred_element_type=jnp.float32)  19.5 us
  transfers between devices with their start and end apart: 3, of which 3 were waited for; matrix products, arithmetic and copies ran while one was open for 11% of the time, Pallas kernels for 0%

commit v1 on v0

v1 whole, which is shorter than its diff:
```python
import jax
import jax.numpy as jnp
from jax import lax
from jax.experimental import pallas as pl
from jax.experimental.pallas import tpu as pltpu
from jax.sharding import Mesh
from jax.sharding import PartitionSpec as P

bf16 = jnp.bfloat16
f32 = jnp.float32

PARTS = ("z", "y2", "y1", "y0", "x1", "x0", "zl", "c")
SIZES = (2, 2, 2, 2, 2, 2, 4, 2)
DP = PARTS[:6]
TENSOR = PARTS[6:]
SWAP = [(0, 1), (1, 0)]
ORDER = ("x0", "y0", "x1", "y1", "y2", "z")
VMEM = pl.BlockSpec(memory_space=pltpu.VMEM)
ANY = pl.BlockSpec(memory_space=pl.ANY)
SMEM = pl.BlockSpec(memory_space=pltpu.SMEM)

ERF = (
    7.97884332e-01,
    3.63339859e-02,
    -3.29015638e-05,
    -5.53135740e-05,
    3.98006372e-06,
    -1.34189628e-07,
    1.82394749e-09,
)


def gelu(x):
    u = x * x
    g = ERF[-1]
    for coef in ERF[-2::-1]:
        g = g * u + coef
    half = 0.5 * x
    return half + half * jnp.tanh(x * g)


def near(x):
    return pltpu.with_memory_space_constraint(x, pltpu.VMEM)


def scene_kernel(len_ref, out_ref):
    ends, end = [], 0
    for s in range(8):
        end = end + len_ref[0, s]
        ends.append(end)
    for block in range(16):
        scene = 0
        for s in range(7):
            scene = scene + (block >= ends[s]).astype(jnp.int32)
        out_ref[block] = scene


def scene_of_block(lengths):
    return pl.pallas_call(
        scene_kernel,
        in_specs=[SMEM],
        out_specs=SMEM,
        out_shape=jax.ShapeDtypeStruct((16,), jnp.int32),
        compiler_params=pltpu.CompilerParams(vmem_limit_bytes=2**20),
        cost_estimate=pl.CostEstimate(flops=20 * 10**9, bytes_accessed=64, transcendentals=0),
    )(lengths)


def in_kernel(x_ref, w_ref, p_ref, o_ref):
    width = 256
    x = x_ref[...]
    total = None
    for n in range(w_ref.shape[1] // width):
        part = slice(n * width, (n + 1) * width)
        z = lax.dot_general(
            w_ref[:, part], x, (((0,), (1,)), ((), ())), preferred_element_type=f32
        )
        term = jnp.dot(p_ref[:, part], gelu(z).astype(bf16), preferred_element_type=f32)
        total = term if total is None else total + term
    half = x.shape[0] // 2
    o_ref[0] = total[:, :half].astype(bf16)
    o_ref[1] = total[:, half:].astype(bf16)


def in_project(x, w, p):
    rows, width = x.shape
    hidden = w.shape[1]
    return pl.pallas_call(
        in_kernel,
        in_specs=[VMEM] * 3,
        out_specs=VMEM,
        out_shape=jax.ShapeDtypeStruct((2, p.shape[0], rows // 2), bf16),
        compiler_params=pltpu.CompilerParams(vmem_limit_bytes=32 * 2**20),
        cost_estimate=pl.CostEstimate(
            flops=2 * rows * hidden * (width + 256),
            bytes_accessed=2 * (rows * width + width * hidden),
            transcendentals=rows * hidden,
        ),
    )(near(x), near(w), near(p))


def feature_kernel(scene_ref, o1_ref, o2_ref, i_ref, out_ref, acc):
    core = lax.axis_index("c")
    acc[...] = jnp.zeros(acc.shape, f32)
    for turn, o_ref in enumerate((o1_ref, o2_ref)):
        half = core ^ turn
        for k in range(8):
            cols = slice(k * 128, (k + 1) * 128)
            acc[scene_ref[half * 8 + k]] += lax.dot_general(
                o_ref[:, cols],
                i_ref[half, :, cols],
                (((1,), (1,)), ((), ())),
                preferred_element_type=f32,
            )
    for m in range(4):
        pair = jnp.concatenate([acc[m], acc[m + 4]], axis=1).astype(bf16)
        for t in range(8):
            out_ref[t, 8 * m : 8 * m + 8, :] = pair[8 * t : 8 * t + 8, :]


def features(scene, o1, o2, i):
    return pl.pallas_call(
        feature_kernel,
        in_specs=[SMEM, VMEM, VMEM, VMEM],
        out_specs=VMEM,
        out_shape=jax.ShapeDtypeStruct((8, 32, 128), bf16),
        scratch_shapes=[pltpu.VMEM((8, 64, 64), f32)],
        compiler_params=pltpu.CompilerParams(vmem_limit_bytes=8 * 2**20),
        cost_estimate=pl.CostEstimate(flops=20 * 10**9, bytes_accessed=2**20, transcendentals=0),
    )(scene, near(o1), near(o2), near(i))


def score_kernel(f_ref, q1_ref, q2_ref, out_ref, own, turned, feat):
    group = lax.axis_index("z") * 4 + lax.axis_index("y2") * 2
    total = f_ref[0].astype(f32)
    for t in range(1, 8):
        total = total + f_ref[t].astype(f32)
    own[...] = total
    turned[...] = pltpu.roll(total, 64, 1)
    low = lax.broadcasted_iota(jnp.int32, (4, 128), 1) < 64
    for p in range(4):
        even, odd = pl.ds(2 * p, 4, stride=8), pl.ds(2 * p + 1, 4, stride=8)
        cols = slice(128 * p, 128 * p + 128)
        feat[0:4, cols] = jnp.where(low, own[even, :], turned[odd, :])
        feat[4:8, cols] = jnp.where(low, turned[even, :], own[odd, :])
    f = feat[...].astype(bf16)
    lanes = lax.broadcasted_iota(jnp.int32, (8, 128), 1)
    for t in range(8):
        rows = []
        for b in range(8):
            bits = dict(z=t & 4, y2=t & 2, y1=t & 1, y0=b & 4, x1=b & 2, x0=b & 1)
            row = 0
            for axis in ORDER:
                row = 2 * row + (bits[axis] > 0)
            ref, row = (q1_ref, row) if row < 32 else (q2_ref, row - 32)
            rows.append(ref[16 * row : 16 * row + 16, :])
        x = lax.dot_general(
            f, jnp.concatenate(rows, axis=0), (((1,), (1,)), ((), ())), preferred_element_type=f32
        )
        for axis, width in (("y0", 64), ("x0", 16)):
            other = jnp.where((lanes & width) == 0, pltpu.roll(x, 128 - width, 1), pltpu.roll(x, width, 1))
            x = jnp.where(lax.axis_index(axis) == 1, other, x)
        out_ref[t ^ group] = x


def partial_scores(f, q1, q2):
    return pl.pallas_call(
        score_kernel,
        in_specs=[VMEM] * 3,
        out_specs=VMEM,
        out_shape=jax.ShapeDtypeStruct((8, 8, 128), f32),
        scratch_shapes=[
            pltpu.VMEM((32, 128), f32),
            pltpu.VMEM((32, 128), f32),
            pltpu.VMEM((8, 512), f32),
        ],
        compiler_params=pltpu.CompilerParams(vmem_limit_bytes=8 * 2**20),
        cost_estimate=pl.CostEstimate(flops=2 * 256 * 512 * 1024, bytes_accessed=2**20, transcendentals=0),
    )(f, q1, q2)


def gather(x, axes):
    count = 2 ** len(axes)
    x = lax.all_to_all(jnp.broadcast_to(x[None], (count,) + x.shape), axes, 0, 0)
    return x.reshape((-1,) + x.shape[2:])


NEAR = [(0, 1), (1, 0), (2, 3), (3, 2)]
FAR = [(0, 2), (2, 0), (1, 3), (3, 1)]
tie = lax.optimization_barrier


def local(inputs, up_weight, out_grad, proj_in, proj_out, queries, lengths):
    core = lax.axis_index("c")
    scene, p = tie((scene_of_block(lengths), proj_in.T))
    q = jnp.concatenate([queries, lax.ppermute(queries, "z", SWAP)], axis=0)
    o = lax.dot_general(proj_out, out_grad, (((0,), (1,)), ((), ())), preferred_element_type=f32)
    half = o.shape[1] // 2
    o1 = lax.dynamic_slice_in_dim(o, core * half, half, 1)
    o2 = lax.dynamic_slice_in_dim(o, (1 - core) * half, half, 1)
    o = o1 + lax.ppermute(o2.astype(bf16), "c", SWAP).astype(f32)
    i = in_project(inputs, up_weight, p)

    o, q, i = tie((o, q, i))
    o = o + lax.ppermute(o.astype(bf16), "zl", NEAR).astype(f32)
    o = o + lax.ppermute(o.astype(bf16), "zl", FAR).astype(f32)
    o1 = o.astype(bf16)
    o2 = lax.ppermute(o1, "c", SWAP)
    q = jnp.concatenate([q, lax.ppermute(q, "y2", SWAP)], axis=0)
    q = gather(q, ("x1", "y1"))
    q, o1, o2 = tie((q, o1, o2))
    q = jnp.concatenate([q, lax.ppermute(q, "y0", SWAP)], axis=0)
    f = features(scene, o1, o2, i)
    q, f = tie((q, f))
    q2 = lax.ppermute(q, "x0", SWAP)
    f = lax.all_to_all(f, TENSOR, 0, 0)
    scores = partial_scores(near(f), near(q), near(q2))
    return jnp.sum(lax.all_to_all(scores, TENSOR, 0, 0), axis=0)


def solution(mesh):
    fine = Mesh(mesh.devices.reshape(SIZES), PARTS)
    return jax.shard_map(
        local,
        mesh=fine,
        in_specs=(
            P(DP, None),
            P(None, TENSOR),
            P(DP, TENSOR),
            P(TENSOR, None),
            P(TENSOR, None),
            P(DP, TENSOR),
            P(DP, None),
        ),
        out_specs=P(DP, TENSOR),
        check_vma=False,
    )
```

time: 193 us -> 87.7 us (0.45)
  waiting for transfers between devices: 113 us -> 10.7 us
  starting transfers between devices: 0.09 us -> 39.8 us
  matrix products: 25.8 us -> 1 us
  blocking collectives: 36.4 us -> 21.3 us
  between operations: 14.9 us -> 0.28 us
  Pallas kernels: 0 us -> 9.77 us
  local copies, waits for them, and re-layouts: 0.21 us -> 2.53 us
    all_gather x1 -> x0, waiting for transfers between devices: 51.7 us -> none  [local(): lax.all_gather(queries, 'dp', axis=0, tiled=True)]
    psum x1 -> x0, blocking collectives: 36.4 us -> none  [local(): in_proj, out_proj = lax.psum((in_part, out_part), 'tensor')]
    ppermute x0 -> x8, starting transfers between devices: none -> 35.6 us  [the longest x1 9.05 us: local(): o = o1 + lax.ppermute(o2.astype(bf16), 'c', SWAP).astype(f32)]
    reduce_scatter x1 -> x0, waiting for transfers between devices: 34.4 us -> none  [local(): lax.psum_scatter(partial_scores, 'tensor', scatter_dimension=1, tiled=True)]
    psum x1 -> x0, waiting for transfers between devices: 26.5 us -> none  [local(): in_proj, out_proj = lax.psum((in_part, out_part), 'tensor')]
    dot_general x4 -> x1, matrix products: 25.8 us -> 1 us  [local(): lax.dot_general(proj_out, out_grad, (((0,), (1,)), ((), ())), preferred_e...]
    all_to_all x0 -> x2, blocking collectives: none -> 21.3 us  [the longest x1 11.8 us: local(): f = lax.all_to_all(f, TENSOR, 0, 0)]
    pallas_call x0 -> x4, Pallas kernels: none -> 9.77 us  [the longest x1 7.02 us: in_project(): pl.pallas_call(in_kernel, in_specs=[VMEM] * 3, out_specs=VMEM, out_shape=...]
  transfers between devices with their start and end apart: 3 -> 9, of which waited for: 3 -> 4; matrix products, arithmetic and copies ran while one was open for 11% -> 1% of each run, Pallas kernels for 0% -> 11%
where the time goes in v1:
time: 87.7 us; the launch traced here: 86.2 us
  starting transfers between devices  39.8 us (45%)
  blocking collectives  21.3 us (24%)
  waiting for transfers between devices  10.7 us (12%)
  Pallas kernels  9.77 us (11%)
  local copies, waits for them, and re-layouts  2.53 us (3%)
  matrix products  1 us (1%)
    all_to_all x1, blocking collectives, local(): f = lax.all_to_all(f, TENSOR, 0, 0)  11.8 us
    all_to_all x1, blocking collectives, local(): return jnp.sum(lax.all_to_all(scores, TENSOR, 0, 0), axis=0)  9.53 us
    ppermute x1, starting transfers between devices, local(): o = o1 + lax.ppermute(o2.astype(bf16), 'c', SWAP).astype(f32)  9.05 us
    ppermute x1, starting transfers between devices, local(): q = jnp.concatenate([q, lax.ppermute(q, 'y2', SWAP)], axis=0)  7.46 us
    pallas_call x1, Pallas kernels, in_project(): pl.pallas_call(in_kernel, in_specs=[VMEM] * 3, out_specs=VMEM, out_shape=...  7.02 us
    ppermute x1, starting transfers between devices, local(): q = jnp.concatenate([queries, lax.ppermute(queries, 'z', SWAP)], axis=0)  5.4 us
    ppermute x1, waiting for transfers between devices, local(): q = jnp.concatenate([q, lax.ppermute(q, 'y0', SWAP)], axis=0)  4.26 us
    all_to_all x1, starting transfers between devices, gather(): lax.all_to_all(jnp.broadcast_to(x[None], (count,) + x.shape), axes, 0, 0)  4.23 us
  transfers between devices with their start and end apart: 9, of which 4 were waited for; matrix products, arithmetic and copies ran while one was open for 1% of the time, Pallas kernels for 11%

profile of v1, /device:TPU:1, one launch (start us, length us, event | category | flops | bytes accessed | tf_op | source)
XLA Modules:
  0.0 86.2 jit_solution(12591482240531729964)
XLA Ops:
  0.0 0.0 copy-start
  0.0 1.1 %copy-done = bf16[2048,176]{0,1:T(8,128)(2,1)S(1)} copy-done((bf16[2048,176]{0,1:T(8,128)(2,1)S(1)}, bf16[2048,176]{0,1:T(8,128)(2,1)}, u32[]{:S(2)}) %copy-start) | copy-done | bytes 720920
  1.1 1.0 %fusion.1 = f32[64,2048]{1,0:T(8,128)S(1)} fusion(bf16[176,64]{0,1:T(8,128)(2,1)} %param.11, bf16[2048,176]{0,1:T(8,128)(2,1)S(1)} %copy-done), kind=kOutput, calls=%fused_computation.8 | convolution fusion | flops 46137344 | bytes 1267712 | tf_op jit(solution)/shard_map/dot_general | solution.py:197
  2.1 0.0 slice-start
  2.2 0.0 slice-start.1
  2.2 0.0 copy-start.1
  2.2 0.0 copy-start.2
  2.2 9.1 %collective-permute-start = (bf16[64,1024]{1,0:T(8,128)(2,1)S(1)}, bf16[64,1024]{1,0:T(8,128)(2,1)S(1)}, u32[]{:S(2)}, u32[]{:S(2)}) collective-permute-start(bf16[64,1024]{1,0:T(8,128)(2,1)S(1)} %dynamic-slice_convert_fusion), channel_id=1, source_target_pairs={{0,1},{1,0},{2,3},{3,2},{4,5},{5,4},{6,7},{7,6},{8,9},{9,8},{10,11... | collective-permute-start | bytes 393224 | tf_op jit(solution)/shard_map/ppermute | solution.py:201
  11.3 5.4 %collective-permute-start.1 = (bf16[16,512]{1,0:T(8,128)(2,1)}, bf16[16,512]{1,0:T(8,128)(2,1)S(1)}, u32[]{:S(2)}, u32[]{:S(2)}) collective-permute-start(bf16[16,512]{1,0:T(8,128)(2,1)} %param.12), channel_id=1, source_target_pairs={{0,256},{256,0},{1,257},{257,1},{2,258},{258,2},{3,259},{259,3},{4... | collective-permute-start | bytes 49160 | tf_op jit(solution)/shard_map/ppermute | solution.py:196
  16.7 0.0 copy-start.3
  16.7 0.6 copy-done.3
  17.3 1.3 %shard_map.73.scene_ref = s32[16]{0:T(128)S(1)} custom-call(s32[1,8]{1,0:T(1,128)S(1)} %copy-done.3), custom_call_target="tpu_custom_call" | custom-call | flops 20000000000 | bytes 64 | tf_op jit(solution)/shard_map/pallas_call | solution.py:59
  18.6 0.0 slice-done
  18.6 0.0 slice-done.1
  18.6 0.0 copy-done.1
  18.6 0.0 copy-done.2
  18.6 0.0 copy-start.4
  18.7 7.0 %shard_map.74.i_ref = bf16[2,64,1024]{2,1,0:T(8,128)(2,1)S(1)} custom-call(bf16[2048,1408]{1,0:T(8,128)(2,1)S(1)} %bitcast.5, bf16[1408,768]{1,0:T(8,128)(2,1)S(1)} %copy-done.1, bf16[64,768]{1,0:T(8,128)(2,1)S(1)} %bitcast.6), custom_call_target="tpu_custom_call" | custom-call | flops 5234491392 | bytes 7929856 | tf_op jit(solution)/shard_map/pallas_call | solution.py:88
  25.7 0.0 collective-permute-done.1
  25.7 0.0 copy-done.4
  25.7 0.0 collective-permute-done
  25.8 3.1 %collective-permute-start.3 = (bf16[64,1024]{1,0:T(8,128)(2,1)S(1)}, bf16[64,1024]{1,0:T(8,128)(2,1)S(1)}, u32[]{:S(2)}, u32[]{:S(2)}) collective-permute-start(bf16[64,1024]{1,0:T(8,128)(2,1)S(1)} %convert_element_type.23), channel_id=1, source_target_pairs={{0,2},{2,0},{4,6},{6,4},{1,3},{3,1},{5,7},{7,5},{8,10},{10,8},{12,... | collective-permute-start | bytes 393224 | tf_op jit(solution)/shard_map/ppermute | solution.py:205
  28.9 7.5 %collective-permute-start.2 = (bf16[32,512]{1,0:T(8,128)(2,1)S(1)}, bf16[32,512]{1,0:T(8,128)(2,1)S(1)}, u32[]{:S(2)}, u32[]{:S(2)}) collective-permute-start(bf16[32,512]{1,0:T(8,128)(2,1)S(1)} %pad_maximum_fusion.2), channel_id=1, source_target_pairs={{0,128},{128,0},{1,129},{129,1},{2,130},{130,2},{3,131},{131,3},{4... | collective-permute-start | bytes 98312 | tf_op jit(solution)/shard_map/ppermute | solution.py:209
  36.4 0.0 collective-permute-done.3
  36.4 4.0 %collective-permute-start.4 = (bf16[64,1024]{1,0:T(8,128)(2,1)S(1)}, bf16[64,1024]{1,0:T(8,128)(2,1)S(1)}, u32[]{:S(2)}, u32[]{:S(2)}) collective-permute-start(bf16[64,1024]{1,0:T(8,128)(2,1)S(1)} %fusion), channel_id=1, source_target_pairs={{0,4},{4,0},{2,6},{6,2},{1,5},{5,1},{3,7},{7,3},{8,12},{12,8},{10,... | collective-permute-start | bytes 393224 | tf_op jit(solution)/shard_map/ppermute | solution.py:206
  40.4 0.0 collective-permute-done.2
  40.5 0.7 broadcast_in_dim.2
  41.2 4.2 %all-to-all-start = ((bf16[4,64,512]{2,1,0:T(8,128)(2,1)}), bf16[4,64,512]{2,1,0:T(8,128)(2,1)S(1)}, u32[]{:S(2)}, u32[]{:S(2)}) async-start(bf16[4,64,512]{2,1,0:T(8,128)(2,1)} %broadcast_in_dim.2), calls=%async_computation | async-start | bytes 524288 | tf_op jit(solution)/shard_map/all_to_all | solution.py:184
  45.4 2.0 %collective-permute-done.4 = bf16[64,1024]{1,0:T(8,128)(2,1)S(1)} collective-permute-done((bf16[64,1024]{1,0:T(8,128)(2,1)S(1)}, bf16[64,1024]{1,0:T(8,128)(2,1)S(1)}, u32[]{:S(2)}, u32[]{:S(2)}) %collective-permute-start.4) | collective-permute-done | bytes 131104 | tf_op jit(solution)/shard_map/ppermute | solution.py:206
  47.4 0.1 add_convert_fusion.o1_ref
  47.5 2.4 %collective-permute-start.5 = (bf16[64,1024]{1,0:T(8,128)(2,1)S(1)}, bf16[64,1024]{1,0:T(8,128)(2,1)S(1)}, u32[]{:S(2)}, u32[]{:S(2)}) collective-permute-start(bf16[64,1024]{1,0:T(8,128)(2,1)S(1)} %add_convert_fusion.o1_ref), channel_id=1, source_target_pairs={{0,1},{1,0},{2,3},{3,2},{4,5},{5,4},{6,7},{7,6},{8,9},{9,8},{10,11... | collective-permute-start | bytes 393224 | tf_op jit(solution)/shard_map/ppermute | solution.py:208
  49.9 1.0 %collective-permute-done.5.o2_ref = bf16[64,1024]{1,0:T(8,128)(2,1)S(1)} collective-permute-done((bf16[64,1024]{1,0:T(8,128)(2,1)S(1)}, bf16[64,1024]{1,0:T(8,128)(2,1)S(1)}, u32[]{:S(2)}, u32[]{:S(2)}) %collective-permute-start.5) | collective-permute-done | bytes 131104 | tf_op jit(solution)/shard_map/ppermute | solution.py:208
  50.8 3.5 %all-to-all-done = bf16[4,64,512]{2,1,0:T(8,128)(2,1)S(1)} async-done(((bf16[4,64,512]{2,1,0:T(8,128)(2,1)}), bf16[4,64,512]{2,1,0:T(8,128)(2,1)S(1)}, u32[]{:S(2)}, u32[]{:S(2)}) %all-to-all-start) | async-done | bytes 262176 | tf_op jit(solution)/shard_map/all_to_all | solution.py:184
  54.3 1.9 %collective-permute-start.6 = (bf16[256,512]{1,0:T(8,128)(2,1)S(1)}, bf16[256,512]{1,0:T(8,128)(2,1)S(1)}, u32[]{:S(2)}, u32[]{:S(2)}) collective-permute-start(bf16[256,512]{1,0:T(8,128)(2,1)S(1)} %bitcast.7), channel_id=1, source_target_pairs={{0,32},{32,0},{1,33},{33,1},{2,34},{34,2},{3,35},{35,3},{4,36},{36... | collective-permute-start | bytes 786440 | tf_op jit(solution)/shard_map/ppermute | solution.py:212
  56.2 0.9 %shard_map.75 = bf16[8,32,128]{2,1,0:T(8,128)(2,1)S(1)} custom-call(s32[16]{0:T(128)S(1)} %shard_map.73.scene_ref, bf16[64,1024]{1,0:T(8,128)(2,1)S(1)} %add_convert_fusion.o1_ref, bf16[64,1024]{1,0:T(8,128)(2,1)S(1)} %collective-permute-done.5.o2_ref, bf16[2,64,1024]{2,1,0:T(8,128)(2,1)S(1)} %shard_map.74.i_ref), custom_call_target="tpu_custom_call" | custom-call | flops 20000000000 | bytes 1048576 | tf_op jit(solution)/shard_map/pallas_call | solution.py:122
  57.1 4.3 %collective-permute-done.6 = bf16[256,512]{1,0:T(8,128)(2,1)S(1)} collective-permute-done((bf16[256,512]{1,0:T(8,128)(2,1)S(1)}, bf16[256,512]{1,0:T(8,128)(2,1)S(1)}, u32[]{:S(2)}, u32[]{:S(2)}) %collective-permute-start.6) | collective-permute-done | bytes 262176 | tf_op jit(solution)/shard_map/ppermute | solution.py:212
  61.4 2.3 %collective-permute-start.7 = (bf16[512,512]{1,0:T(8,128)(2,1)S(1)}, bf16[512,512]{1,0:T(8,128)(2,1)S(1)}, u32[]{:S(2)}, u32[]{:S(2)}) collective-permute-start(bf16[512,512]{1,0:T(8,128)(2,1)S(1)} %pad_maximum_fusion.q1_ref), channel_id=1, source_target_pairs={{0,8},{8,0},{1,9},{9,1},{2,10},{10,2},{3,11},{11,3},{4,12},{12,4},... | collective-permute-start | bytes 1572872 | tf_op jit(solution)/shard_map/ppermute | solution.py:215
  63.7 11.8 %all_to_all.15.f_ref = bf16[8,32,128]{2,1,0:T(8,128)(2,1)S(1)} all-to-all(bf16[8,32,128]{2,1,0:T(8,128)(2,1)S(1)} %shard_map.75), channel_id=1, replica_groups=mesh['z'=2,'y2'=2,'y1'=2,'y0'=2,'x1'=2,'x0'=2,'zl'=4,'c'=2] {'zl','c'}, dimensions={0} | all-to-all | bytes 131072 | tf_op jit(solution)/shard_map/all_to_all | solution.py:216
  75.5 0.0 collective-permute-done.7.q2_ref
  75.5 0.6 shard_map.76
  76.1 9.5 %all_to_all.16 = f32[8,8,128]{2,1,0:T(8,128)S(1)} all-to-all(f32[8,8,128]{2,1,0:T(8,128)S(1)} %shard_map.76), channel_id=1, replica_groups=mesh['z'=2,'y2'=2,'y1'=2,'y0'=2,'x1'=2,'x0'=2,'zl'=4,'c'=2] {'zl','c'}, dimensions={0} | all-to-all | bytes 65536 | tf_op jit(solution)/shard_map/all_to_all | solution.py:218
  85.6 0.6 reduce_sum.9
  (8 shorter events, 0.2 us)
Async XLA Ops:
  0.0 1.1 %copy-start = (bf16[2048,176]{0,1:T(8,128)(2,1)S(1)}, bf16[2048,176]{0,1:T(8,128)(2,1)}, u32[]{:S(2)}) copy-start(bf16[2048,176]{0,1:T(8,128)(2,1)} %param.9) | copy-start | bytes 2162692
  2.1 16.5 %slice-start = ((s8[5767168]{0:T(1024)(128)(4,1)}), s8[4194304]{0:T(1024)(128)(4,1)S(1)}, s32[]{:S(2)}) async-start(s8[5767168]{0:T(1024)(128)(4,1)} %bitcast.4), calls=%async_computation.3 | async-start | bytes 8388608
  2.2 16.4 %slice-start.1 = ((s8[5767168]{0:T(1024)(128)(4,1)}), s8[1572864]{0:T(1024)(128)(4,1)S(1)}, s32[]{:S(2)}) async-start(s8[5767168]{0:T(1024)(128)(4,1)} %bitcast.4), calls=%async_computation.4 | async-start | bytes 3145728
  2.2 16.4 %copy-start.1 = (bf16[1408,768]{1,0:T(8,128)(2,1)S(1)}, bf16[1408,768]{1,0:T(8,128)(2,1)}, u32[]{:S(2)}) copy-start(bf16[1408,768]{1,0:T(8,128)(2,1)} %w_ref.1) | copy-start | bytes 6488068
  2.2 16.4 %copy-start.2 = (bf16[768,64]{0,1:T(8,128)(2,1)S(1)}, bf16[768,64]{0,1:T(8,128)(2,1)}, u32[]{:S(2)}) copy-start(bf16[768,64]{0,1:T(8,128)(2,1)} %param.10) | copy-start | bytes 294916
  2.2 23.5 %collective-permute-start = (bf16[64,1024]{1,0:T(8,128)(2,1)S(1)}, bf16[64,1024]{1,0:T(8,128)(2,1)S(1)}, u32[]{:S(2)}, u32[]{:S(2)}) collective-permute-start(bf16[64,1024]{1,0:T(8,128)(2,1)S(1)} %dynamic-slice_convert_fusion), channel_id=1, source_target_pairs={{0,1},{1,0},{2,3},{3,2},{4,5},{5,4},{6,7},{7,6},{8,9},{9,8},{10,11... | collective-permute-start | bytes 393224 | tf_op jit(solution)/shard_map/ppermute | solution.py:201
  11.3 14.4 %collective-permute-start.1 = (bf16[16,512]{1,0:T(8,128)(2,1)}, bf16[16,512]{1,0:T(8,128)(2,1)S(1)}, u32[]{:S(2)}, u32[]{:S(2)}) collective-permute-start(bf16[16,512]{1,0:T(8,128)(2,1)} %param.12), channel_id=1, source_target_pairs={{0,256},{256,0},{1,257},{257,1},{2,258},{258,2},{3,259},{259,3},{4... | collective-permute-start | bytes 49160 | tf_op jit(solution)/shard_map/ppermute | solution.py:196
  16.7 0.7 copy-start.3
  18.6 7.0 %copy-start.4 = (bf16[16,512]{1,0:T(8,128)(2,1)S(1)}, bf16[16,512]{1,0:T(8,128)(2,1)}, u32[]{:S(2)}) copy-start(bf16[16,512]{1,0:T(8,128)(2,1)} %param.12) | copy-start | bytes 49156
  25.8 10.6 %collective-permute-start.3 = (bf16[64,1024]{1,0:T(8,128)(2,1)S(1)}, bf16[64,1024]{1,0:T(8,128)(2,1)S(1)}, u32[]{:S(2)}, u32[]{:S(2)}) collective-permute-start(bf16[64,1024]{1,0:T(8,128)(2,1)S(1)} %convert_element_type.23), channel_id=1, source_target_pairs={{0,2},{2,0},{4,6},{6,4},{1,3},{3,1},{5,7},{7,5},{8,10},{10,8},{12,... | collective-permute-start | bytes 393224 | tf_op jit(solution)/shard_map/ppermute | solution.py:205
  28.9 11.5 %collective-permute-start.2 = (bf16[32,512]{1,0:T(8,128)(2,1)S(1)}, bf16[32,512]{1,0:T(8,128)(2,1)S(1)}, u32[]{:S(2)}, u32[]{:S(2)}) collective-permute-start(bf16[32,512]{1,0:T(8,128)(2,1)S(1)} %pad_maximum_fusion.2), channel_id=1, source_target_pairs={{0,128},{128,0},{1,129},{129,1},{2,130},{130,2},{3,131},{131,3},{4... | collective-permute-start | bytes 98312 | tf_op jit(solution)/shard_map/ppermute | solution.py:209
  36.4 11.0 %collective-permute-start.4 = (bf16[64,1024]{1,0:T(8,128)(2,1)S(1)}, bf16[64,1024]{1,0:T(8,128)(2,1)S(1)}, u32[]{:S(2)}, u32[]{:S(2)}) collective-permute-start(bf16[64,1024]{1,0:T(8,128)(2,1)S(1)} %fusion), channel_id=1, source_target_pairs={{0,4},{4,0},{2,6},{6,2},{1,5},{5,1},{3,7},{7,3},{8,12},{12,8},{10,... | collective-permute-start | bytes 393224 | tf_op jit(solution)/shard_map/ppermute | solution.py:206
  41.2 13.1 %all-to-all-start = ((bf16[4,64,512]{2,1,0:T(8,128)(2,1)}), bf16[4,64,512]{2,1,0:T(8,128)(2,1)S(1)}, u32[]{:S(2)}, u32[]{:S(2)}) async-start(bf16[4,64,512]{2,1,0:T(8,128)(2,1)} %broadcast_in_dim.2), calls=%async_computation | async-start | bytes 524288 | tf_op jit(solution)/shard_map/all_to_all | solution.py:184
  47.5 3.4 %collective-permute-start.5 = (bf16[64,1024]{1,0:T(8,128)(2,1)S(1)}, bf16[64,1024]{1,0:T(8,128)(2,1)S(1)}, u32[]{:S(2)}, u32[]{:S(2)}) collective-permute-start(bf16[64,1024]{1,0:T(8,128)(2,1)S(1)} %add_convert_fusion.o1_ref), channel_id=1, source_target_pairs={{0,1},{1,0},{2,3},{3,2},{4,5},{5,4},{6,7},{7,6},{8,9},{9,8},{10,11... | collective-permute-start | bytes 393224 | tf_op jit(solution)/shard_map/ppermute | solution.py:208
  54.3 7.1 %collective-permute-start.6 = (bf16[256,512]{1,0:T(8,128)(2,1)S(1)}, bf16[256,512]{1,0:T(8,128)(2,1)S(1)}, u32[]{:S(2)}, u32[]{:S(2)}) collective-permute-start(bf16[256,512]{1,0:T(8,128)(2,1)S(1)} %bitcast.7), channel_id=1, source_target_pairs={{0,32},{32,0},{1,33},{33,1},{2,34},{34,2},{3,35},{35,3},{4,36},{36... | collective-permute-start | bytes 786440 | tf_op jit(solution)/shard_map/ppermute | solution.py:212
  61.4 14.1 %collective-permute-start.7 = (bf16[512,512]{1,0:T(8,128)(2,1)S(1)}, bf16[512,512]{1,0:T(8,128)(2,1)S(1)}, u32[]{:S(2)}, u32[]{:S(2)}) collective-permute-start(bf16[512,512]{1,0:T(8,128)(2,1)S(1)} %pad_maximum_fusion.q1_ref), channel_id=1, source_target_pairs={{0,8},{8,0},{1,9},{9,1},{2,10},{10,2},{3,11},{11,3},{4,12},{12,4},... | collective-permute-start | bytes 1572872 | tf_op jit(solution)/shard_map/ppermute | solution.py:215

commit v2 on v1

--- a/solution.py
+++ b/solution.py
@@ -14,7 +14,7 @@
 DP = PARTS[:6]
 TENSOR = PARTS[6:]
 SWAP = [(0, 1), (1, 0)]
-ORDER = ("x0", "y0", "x1", "y1", "y2", "z")
+ORDER = ("y0", "x0", "y1", "x1", "y2", "z")
 VMEM = pl.BlockSpec(memory_space=pltpu.VMEM)
 ANY = pl.BlockSpec(memory_space=pl.ANY)
 SMEM = pl.BlockSpec(memory_space=pltpu.SMEM)
@@ -99,7 +99,7 @@
     )(near(x), near(w), near(p))
 
 
-def feature_kernel(scene_ref, o1_ref, o2_ref, i_ref, out_ref, acc):
+def feature_kernel(scene_ref, o1_ref, o2_ref, i_ref, keep_ref, sent_ref, acc):
     core = lax.axis_index("c")
     acc[...] = jnp.zeros(acc.shape, f32)
     for turn, o_ref in enumerate((o1_ref, o2_ref)):
@@ -113,28 +113,30 @@
                 preferred_element_type=f32,
             )
     for m in range(4):
-        pair = jnp.concatenate([acc[m], acc[m + 4]], axis=1).astype(bf16)
-        for t in range(8):
-            out_ref[t, 8 * m : 8 * m + 8, :] = pair[8 * t : 8 * t + 8, :]
+        pair = jnp.concatenate([acc[m], acc[m + 4]], axis=1)
+        for t in range(4):
+            even = pair[16 * t : 16 * t + 8, :]
+            odd = pair[16 * t + 8 : 16 * t + 16, :]
+            keep_ref[t, 8 * m : 8 * m + 8, :] = jnp.where(core == 0, even, odd)
+            sent_ref[t, 8 * m : 8 * m + 8, :] = jnp.where(core == 0, odd, even).astype(bf16)
 
 
 def features(scene, o1, o2, i):
     return pl.pallas_call(
         feature_kernel,
         in_specs=[SMEM, VMEM, VMEM, VMEM],
-        out_specs=VMEM,
-        out_shape=jax.ShapeDtypeStruct((8, 32, 128), bf16),
+        out_specs=[VMEM, VMEM],
+        out_shape=[jax.ShapeDtypeStruct((4, 32, 128), f32), jax.ShapeDtypeStruct((4, 32, 128), bf16)],
         scratch_shapes=[pltpu.VMEM((8, 64, 64), f32)],
         compiler_params=pltpu.CompilerParams(vmem_limit_bytes=8 * 2**20),
-        cost_estimate=pl.CostEstimate(flops=20 * 10**9, bytes_accessed=2**20, transcendentals=0),
+        cost_estimate=pl.CostEstimate(flops=2 * 10**8, bytes_accessed=2**20, transcendentals=0),
     )(scene, near(o1), near(o2), near(i))
 
 
-def score_kernel(f_ref, q1_ref, q2_ref, out_ref, own, turned, feat):
-    group = lax.axis_index("z") * 4 + lax.axis_index("y2") * 2
-    total = f_ref[0].astype(f32)
-    for t in range(1, 8):
-        total = total + f_ref[t].astype(f32)
+def score_kernel(f1_ref, f2_ref, q_ref, out_ref, own, turned, feat):
+    group = lax.axis_index("z") * 4 + lax.axis_index("y2") * 2 + lax.axis_index("y1")
+    lanes = lax.broadcasted_iota(jnp.int32, (8, 128), 1)
+    total = f1_ref[...] + f2_ref[...].astype(f32)
     own[...] = total
     turned[...] = pltpu.roll(total, 64, 1)
     low = lax.broadcasted_iota(jnp.int32, (4, 128), 1) < 64
@@ -144,7 +146,6 @@
         feat[0:4, cols] = jnp.where(low, own[even, :], turned[odd, :])
         feat[4:8, cols] = jnp.where(low, turned[even, :], own[odd, :])
     f = feat[...].astype(bf16)
-    lanes = lax.broadcasted_iota(jnp.int32, (8, 128), 1)
     for t in range(8):
         rows = []
         for b in range(8):
@@ -152,18 +153,15 @@
             row = 0
             for axis in ORDER:
                 row = 2 * row + (bits[axis] > 0)
-            ref, row = (q1_ref, row) if row < 32 else (q2_ref, row - 32)
-            rows.append(ref[16 * row : 16 * row + 16, :])
+            rows.append(q_ref[16 * row : 16 * row + 16, :])
         x = lax.dot_general(
             f, jnp.concatenate(rows, axis=0), (((1,), (1,)), ((), ())), preferred_element_type=f32
         )
-        for axis, width in (("y0", 64), ("x0", 16)):
-            other = jnp.where((lanes & width) == 0, pltpu.roll(x, 128 - width, 1), pltpu.roll(x, width, 1))
-            x = jnp.where(lax.axis_index(axis) == 1, other, x)
-        out_ref[t ^ group] = x
-
-
-def partial_scores(f, q1, q2):
+        other = jnp.where((lanes & 32) == 0, pltpu.roll(x, 96, 1), pltpu.roll(x, 32, 1))
+        out_ref[t ^ group] = jnp.where(lax.axis_index("x1") == 1, other, x)
+
+
+def partial_scores(f1, f2, q):
     return pl.pallas_call(
         score_kernel,
         in_specs=[VMEM] * 3,
@@ -176,7 +174,7 @@
         ],
         compiler_params=pltpu.CompilerParams(vmem_limit_bytes=8 * 2**20),
         cost_estimate=pl.CostEstimate(flops=2 * 256 * 512 * 1024, bytes_accessed=2**20, transcendentals=0),
-    )(f, q1, q2)
+    )(near(f1), near(f2), near(q))
 
 
 def gather(x, axes):
@@ -199,22 +197,32 @@
     o1 = lax.dynamic_slice_in_dim(o, core * half, half, 1)
     o2 = lax.dynamic_slice_in_dim(o, (1 - core) * half, half, 1)
     o = o1 + lax.ppermute(o2.astype(bf16), "c", SWAP).astype(f32)
+
     i = in_project(inputs, up_weight, p)
 
     o, q, i = tie((o, q, i))
-    o = o + lax.ppermute(o.astype(bf16), "zl", NEAR).astype(f32)
+    q2 = lax.ppermute(q, "y2", SWAP)
+    o2 = lax.ppermute(o.astype(bf16), "zl", NEAR)
+    o, o2, q, q2 = tie((o, o2, q, q2))
+    q = jnp.concatenate([q, q2], axis=0)
+    q = jnp.concatenate([q, lax.ppermute(q, "x1", SWAP)], axis=0)
+    q = jnp.concatenate([q, lax.ppermute(q, "y1", SWAP)], axis=0)
+    o = o + o2.astype(f32)
     o = o + lax.ppermute(o.astype(bf16), "zl", FAR).astype(f32)
     o1 = o.astype(bf16)
     o2 = lax.ppermute(o1, "c", SWAP)
-    q = jnp.concatenate([q, lax.ppermute(q, "y2", SWAP)], axis=0)
-    q = gather(q, ("x1", "y1"))
-    q, o1, o2 = tie((q, o1, o2))
-    q = jnp.concatenate([q, lax.ppermute(q, "y0", SWAP)], axis=0)
-    f = features(scene, o1, o2, i)
+
+    f, sent = features(scene, o1, o2, i)
+    f = f + lax.ppermute(sent, "c", SWAP).astype(f32)
     q, f = tie((q, f))
-    q2 = lax.ppermute(q, "x0", SWAP)
-    f = lax.all_to_all(f, TENSOR, 0, 0)
-    scores = partial_scores(near(f), near(q), near(q2))
+    q = gather(q, ("y0", "x0"))
+    f = f.reshape((2, 2) + f.shape[1:])
+    low, high = lax.axis_index("zl") % 2, lax.axis_index("zl") // 2
+    sent = lax.dynamic_index_in_dim(f, 1 - low, 1, False).astype(bf16)
+    f = lax.dynamic_index_in_dim(f, low, 1, False) + lax.ppermute(sent, "zl", NEAR).astype(f32)
+    sent = lax.dynamic_index_in_dim(f, 1 - high, 0, False).astype(bf16)
+    f = lax.dynamic_index_in_dim(f, high, 0, False)
+    scores = partial_scores(f, lax.ppermute(sent, "zl", FAR), q)
     return jnp.sum(lax.all_to_all(scores, TENSOR, 0, 0), axis=0)
 
 

time: 87.7 us -> 90.7 us (1.034)
  starting transfers between devices: 39.8 us -> 51.9 us
  blocking collectives: 21.3 us -> 9.89 us
  waiting for transfers between devices: 10.7 us -> 14.5 us
    ppermute x4 -> x7, starting transfers between devices: 14.7 us -> 26.9 us  [the longest x1 7.45 us: local(): q2 = lax.ppermute(q, 'y2', SWAP)]
    all_to_all x1 -> x0, blocking collectives: 11.8 us -> none  [local(): f = lax.all_to_all(f, TENSOR, 0, 0)]
    ppermute x1, starting transfers between devices: 5.4 us -> 11.6 us  [local(): q = jnp.concatenate([queries, lax.ppermute(queries, 'z', SWAP)], axis=0)]
    ppermute x1, starting transfers between devices: 9.05 us -> 3.13 us  [local(): o = o1 + lax.ppermute(o2.astype(bf16), 'c', SWAP).astype(f32)]
    ppermute x4 -> x7, waiting for transfers between devices: 4.27 us -> 9.66 us  [the longest x1 3.36 us: local(): q = jnp.concatenate([q, lax.ppermute(q, 'y1', SWAP)], axis=0)]
    unnamed x14, local copies, waits for them, and re-layouts: 1.79 us -> 0.69 us
    ppermute x1, waiting for transfers between devices: 0.96 us -> 0.01 us  [local(): o2 = lax.ppermute(o1, 'c', SWAP)]
  transfers between devices with their start and end apart: 9 -> 12, of which waited for: 4 -> 6; matrix products, arithmetic and copies ran while one was open for 1% -> 1% of each run, Pallas kernels for 11% -> 10%
where the time goes in v2:
time: 90.7 us; the launch traced here: 90.1 us
  starting transfers between devices  51.9 us (57%)
  waiting for transfers between devices  14.5 us (16%)
  blocking collectives  9.89 us (11%)
  Pallas kernels  9.7 us (11%)
  local copies, waits for them, and re-layouts  1.82 us (2%)
  matrix products  1 us (1%)
    ppermute x1, starting transfers between devices, local(): q = jnp.concatenate([queries, lax.ppermute(queries, 'z', SWAP)], axis=0)  11.6 us
    all_to_all x1, blocking collectives, local(): return jnp.sum(lax.all_to_all(scores, TENSOR, 0, 0), axis=0)  9.89 us
    ppermute x1, starting transfers between devices, local(): q2 = lax.ppermute(q, 'y2', SWAP)  7.45 us
    pallas_call x1, Pallas kernels, in_project(): pl.pallas_call(in_kernel, in_specs=[VMEM] * 3, out_specs=VMEM, out_shape=...  7.02 us
    ppermute x1, starting transfers between devices, local(): q = jnp.concatenate([q, lax.ppermute(q, 'x1', SWAP)], axis=0)  4.67 us
    ppermute x1, starting transfers between devices, local(): q = jnp.concatenate([q, lax.ppermute(q, 'y1', SWAP)], axis=0)  4.41 us
    ppermute x1, starting transfers between devices, local(): o = o + lax.ppermute(o.astype(bf16), 'zl', FAR).astype(f32)  4.01 us
    all_to_all x1, starting transfers between devices, gather(): lax.all_to_all(jnp.broadcast_to(x[None], (count,) + x.shape), axes, 0, 0)  3.51 us
  transfers between devices with their start and end apart: 12, of which 6 were waited for; matrix products, arithmetic and copies ran while one was open for 1% of the time, Pallas kernels for 10%

profile of v2, /device:TPU:1, one launch (start us, length us, event | category | flops | bytes accessed | tf_op | source)
XLA Modules:
  0.0 90.1 jit_solution(3702439942544037828)
XLA Ops:
  0.0 0.0 copy-start
  0.0 11.6 %collective-permute-start.1 = (bf16[16,512]{1,0:T(8,128)(2,1)}, bf16[16,512]{1,0:T(8,128)(2,1)S(1)}, u32[]{:S(2)}, u32[]{:S(2)}) collective-permute-start(bf16[16,512]{1,0:T(8,128)(2,1)} %param.12), channel_id=1, source_target_pairs={{0,256},{256,0},{1,257},{257,1},{2,258},{258,2},{3,259},{259,3},{4... | collective-permute-start | bytes 49160 | tf_op jit(solution)/shard_map/ppermute | solution.py:194
  11.6 0.0 copy-done
  11.6 1.0 %fusion.3 = f32[64,2048]{1,0:T(8,128)S(1)} fusion(bf16[176,64]{0,1:T(8,128)(2,1)} %param.11, bf16[2048,176]{0,1:T(8,128)(2,1)S(1)} %copy-done), kind=kOutput, calls=%fused_computation.16 | convolution fusion | flops 46137344 | bytes 1267712 | tf_op jit(solution)/shard_map/dot_general | solution.py:195
  12.6 0.0 slice-start
  12.7 0.0 slice-start.1
  12.7 0.0 copy-start.1
  12.7 0.0 copy-start.2
  12.7 3.1 %collective-permute-start = (bf16[64,1024]{1,0:T(8,128)(2,1)S(1)}, bf16[64,1024]{1,0:T(8,128)(2,1)S(1)}, u32[]{:S(2)}, u32[]{:S(2)}) collective-permute-start(bf16[64,1024]{1,0:T(8,128)(2,1)S(1)} %dynamic-slice_convert_fusion), channel_id=1, source_target_pairs={{0,1},{1,0},{2,3},{3,2},{4,5},{5,4},{6,7},{7,6},{8,9},{9,8},{10,11... | collective-permute-start | bytes 393224 | tf_op jit(solution)/shard_map/ppermute | solution.py:199
  15.8 0.0 copy-start.3
  15.9 0.6 copy-done.3
  16.5 1.3 %shard_map.73.scene_ref = s32[16]{0:T(128)S(1)} custom-call(s32[1,8]{1,0:T(1,128)S(1)} %copy-done.3), custom_call_target="tpu_custom_call" | custom-call | flops 20000000000 | bytes 64 | tf_op jit(solution)/shard_map/pallas_call | solution.py:59
  17.8 0.0 slice-done
  17.8 0.0 slice-done.1
  17.8 0.0 copy-done.1
  17.8 0.0 copy-done.2
  17.8 0.0 copy-start.4
  17.8 7.0 %shard_map.74.i_ref = bf16[2,64,1024]{2,1,0:T(8,128)(2,1)S(1)} custom-call(bf16[2048,1408]{1,0:T(8,128)(2,1)S(1)} %bitcast.19, bf16[1408,768]{1,0:T(8,128)(2,1)S(1)} %copy-done.1, bf16[64,768]{1,0:T(8,128)(2,1)S(1)} %bitcast.20), custom_call_target="tpu_custom_call" | custom-call | flops 5234491392 | bytes 7929856 | tf_op jit(solution)/shard_map/pallas_call | solution.py:88
  24.9 0.0 collective-permute-done.1
  24.9 0.0 copy-done.4
  24.9 0.0 collective-permute-done
  25.0 3.1 %collective-permute-start.2 = (bf16[64,1024]{1,0:T(8,128)(2,1)S(1)}, bf16[64,1024]{1,0:T(8,128)(2,1)S(1)}, u32[]{:S(2)}, u32[]{:S(2)}) collective-permute-start(bf16[64,1024]{1,0:T(8,128)(2,1)S(1)} %convert_element_type.41), channel_id=1, source_target_pairs={{0,2},{2,0},{4,6},{6,4},{1,3},{3,1},{5,7},{7,5},{8,10},{10,8},{12,... | collective-permute-start | bytes 393224 | tf_op jit(solution)/shard_map/ppermute | solution.py:205
  28.1 7.5 %collective-permute-start.3 = (bf16[32,512]{1,0:T(8,128)(2,1)S(1)}, bf16[32,512]{1,0:T(8,128)(2,1)S(1)}, u32[]{:S(2)}, u32[]{:S(2)}) collective-permute-start(bf16[32,512]{1,0:T(8,128)(2,1)S(1)} %pad_maximum_fusion.3), channel_id=1, source_target_pairs={{0,128},{128,0},{1,129},{129,1},{2,130},{130,2},{3,131},{131,3},{4... | collective-permute-start | bytes 98312 | tf_op jit(solution)/shard_map/ppermute | solution.py:204
  35.5 1.3 %collective-permute-done.3 = bf16[32,512]{1,0:T(8,128)(2,1)S(1)} collective-permute-done((bf16[32,512]{1,0:T(8,128)(2,1)S(1)}, bf16[32,512]{1,0:T(8,128)(2,1)S(1)}, u32[]{:S(2)}, u32[]{:S(2)}) %collective-permute-start.3) | collective-permute-done | bytes 32800 | tf_op jit(solution)/shard_map/ppermute | solution.py:204
  36.9 0.0 collective-permute-done.2
  36.9 4.0 %collective-permute-start.6 = (bf16[64,1024]{1,0:T(8,128)(2,1)S(1)}, bf16[64,1024]{1,0:T(8,128)(2,1)S(1)}, u32[]{:S(2)}, u32[]{:S(2)}) collective-permute-start(bf16[64,1024]{1,0:T(8,128)(2,1)S(1)} %fusion), channel_id=1, source_target_pairs={{0,4},{4,0},{2,6},{6,2},{1,5},{5,1},{3,7},{7,3},{8,12},{12,8},{10,... | collective-permute-start | bytes 393224 | tf_op jit(solution)/shard_map/ppermute | solution.py:211
  40.9 4.7 %collective-permute-start.4 = (bf16[64,512]{1,0:T(8,128)(2,1)S(1)}, bf16[64,512]{1,0:T(8,128)(2,1)S(1)}, u32[]{:S(2)}, u32[]{:S(2)}) collective-permute-start(bf16[64,512]{1,0:T(8,128)(2,1)S(1)} %pad_maximum_fusion.2), channel_id=1, source_target_pairs={{0,16},{16,0},{1,17},{17,1},{2,18},{18,2},{3,19},{19,3},{4,20},{20... | collective-permute-start | bytes 196616 | tf_op jit(solution)/shard_map/ppermute | solution.py:208
  45.6 1.9 %collective-permute-done.6 = bf16[64,1024]{1,0:T(8,128)(2,1)S(1)} collective-permute-done((bf16[64,1024]{1,0:T(8,128)(2,1)S(1)}, bf16[64,1024]{1,0:T(8,128)(2,1)S(1)}, u32[]{:S(2)}, u32[]{:S(2)}) %collective-permute-start.6) | collective-permute-done | bytes 131104 | tf_op jit(solution)/shard_map/ppermute | solution.py:211
  47.6 2.8 %collective-permute-start.7 = (bf16[64,1024]{1,0:T(8,128)(2,1)S(1)}, bf16[64,1024]{1,0:T(8,128)(2,1)S(1)}, u32[]{:S(2)}, u32[]{:S(2)}) collective-permute-start(bf16[64,1024]{1,0:T(8,128)(2,1)S(1)} %add_convert_fusion.o1_ref), channel_id=1, source_target_pairs={{0,1},{1,0},{2,3},{3,2},{4,5},{5,4},{6,7},{7,6},{8,9},{9,8},{10,11... | collective-permute-start | bytes 393224 | tf_op jit(solution)/shard_map/ppermute | solution.py:213
  50.4 0.0 collective-permute-done.4
  50.4 4.4 %collective-permute-start.5 = (bf16[128,512]{1,0:T(8,128)(2,1)S(1)}, bf16[128,512]{1,0:T(8,128)(2,1)S(1)}, u32[]{:S(2)}, u32[]{:S(2)}) collective-permute-start(bf16[128,512]{1,0:T(8,128)(2,1)S(1)} %pad_maximum_fusion.1), channel_id=1, source_target_pairs={{0,64},{64,0},{1,65},{65,1},{2,66},{66,2},{3,67},{67,3},{4,68},{68... | collective-permute-start | bytes 393224 | tf_op jit(solution)/shard_map/ppermute | solution.py:209
  54.8 0.0 collective-permute-done.7.o2_ref
  54.8 0.9 %shard_map.75 = (f32[4,32,128]{2,1,0:T(8,128)S(1)}, bf16[4,32,128]{2,1,0:T(8,128)(2,1)S(1)}) custom-call(s32[16]{0:T(128)S(1)} %shard_map.73.scene_ref, bf16[64,1024]{1,0:T(8,128)(2,1)S(1)} %add_convert_fusion.o1_ref, bf16[64,1024]{1,0:T(8,128)(2,1)S(1)} %collective-permute-done.7.o2_ref, bf16[2,64,1024]{2,1,0:T(8,128)(2,1)S(1)} %shard_map.74.i_ref), custom_call_target="tpu_custom_call" | custom-call | flops 200000000 | bytes 1048576 | tf_op jit(solution)/shard_map/pallas_call | solution.py:125
  55.8 2.2 %collective-permute-start.8 = (bf16[4,32,128]{2,1,0:T(8,128)(2,1)S(1)}, bf16[4,32,128]{2,1,0:T(8,128)(2,1)S(1)}, u32[]{:S(2)}, u32[]{:S(2)}) collective-permute-start(bf16[4,32,128]{2,1,0:T(8,128)(2,1)S(1)} %get-tuple-element.28), channel_id=1, source_target_pairs={{0,1},{1,0},{2,3},{3,2},{4,5},{5,4},{6,7},{7,6},{8,9},{9,8},{10,11... | collective-permute-start | bytes 98312 | tf_op jit(solution)/shard_map/ppermute | solution.py:216
  58.0 3.4 %collective-permute-done.5 = bf16[128,512]{1,0:T(8,128)(2,1)S(1)} collective-permute-done((bf16[128,512]{1,0:T(8,128)(2,1)S(1)}, bf16[128,512]{1,0:T(8,128)(2,1)S(1)}, u32[]{:S(2)}, u32[]{:S(2)}) %collective-permute-start.5) | collective-permute-done | bytes 131104 | tf_op jit(solution)/shard_map/ppermute | solution.py:209
  61.4 0.0 collective-permute-done.8
  61.4 1.1 %broadcast_in_dim.2 = bf16[4,256,512]{2,1,0:T(8,128)(2,1)} broadcast(bf16[256,512]{1,0:T(8,128)(2,1)S(1)} %pad_maximum_fusion), dimensions={1,2} | broadcast | bytes 1310720 | tf_op jit(solution)/shard_map/broadcast_in_dim | solution.py:182
  62.5 3.5 %all-to-all-start = ((bf16[4,256,512]{2,1,0:T(8,128)(2,1)}), bf16[4,256,512]{2,1,0:T(8,128)(2,1)S(1)}, u32[]{:S(2)}, u32[]{:S(2)}) async-start(bf16[4,256,512]{2,1,0:T(8,128)(2,1)} %broadcast_in_dim.2), calls=%async_computation | async-start | bytes 2097152 | tf_op jit(solution)/shard_map/all_to_all | solution.py:182
  66.0 1.9 %collective-permute-start.9 = (bf16[2,32,128]{2,1,0:T(8,128)(2,1)S(1)}, bf16[2,32,128]{2,1,0:T(8,128)(2,1)S(1)}, u32[]{:S(2)}, u32[]{:S(2)}) collective-permute-start(bf16[2,32,128]{2,1,0:T(8,128)(2,1)S(1)} %fusion.1), channel_id=1, source_target_pairs={{0,2},{2,0},{4,6},{6,4},{1,3},{3,1},{5,7},{7,5},{8,10},{10,8},{12,... | collective-permute-start | bytes 49160 | tf_op jit(solution)/shard_map/ppermute | solution.py:222
  68.0 2.5 %collective-permute-done.9 = bf16[2,32,128]{2,1,0:T(8,128)(2,1)S(1)} collective-permute-done((bf16[2,32,128]{2,1,0:T(8,128)(2,1)S(1)}, bf16[2,32,128]{2,1,0:T(8,128)(2,1)S(1)}, u32[]{:S(2)}, u32[]{:S(2)}) %collective-permute-start.9) | collective-permute-done | bytes 16416 | tf_op jit(solution)/shard_map/ppermute | solution.py:222
  70.5 3.1 %collective-permute-start.10 = (bf16[32,128]{1,0:T(8,128)(2,1)S(1)}, bf16[32,128]{1,0:T(8,128)(2,1)S(1)}, u32[]{:S(2)}, u32[]{:S(2)}) collective-permute-start(bf16[32,128]{1,0:T(8,128)(2,1)S(1)} %fusion.2), channel_id=1, source_target_pairs={{0,4},{4,0},{2,6},{6,2},{1,5},{5,1},{3,7},{7,3},{8,12},{12,8},{10,... | collective-permute-start | bytes 24584 | tf_op jit(solution)/shard_map/ppermute | solution.py:225
  73.7 2.4 %collective-permute-done.10.f2_ref = bf16[32,128]{1,0:T(8,128)(2,1)S(1)} collective-permute-done((bf16[32,128]{1,0:T(8,128)(2,1)S(1)}, bf16[32,128]{1,0:T(8,128)(2,1)S(1)}, u32[]{:S(2)}, u32[]{:S(2)}) %collective-permute-start.10) | collective-permute-done | bytes 8224 | tf_op jit(solution)/shard_map/ppermute | solution.py:225
  76.1 3.0 %all-to-all-done = bf16[4,256,512]{2,1,0:T(8,128)(2,1)S(1)} async-done(((bf16[4,256,512]{2,1,0:T(8,128)(2,1)}), bf16[4,256,512]{2,1,0:T(8,128)(2,1)S(1)}, u32[]{:S(2)}, u32[]{:S(2)}) %all-to-all-start) | async-done | bytes 1048608 | tf_op jit(solution)/shard_map/all_to_all | solution.py:182
  79.1 0.5 shard_map.76
  79.6 9.9 %all_to_all.10 = f32[8,8,128]{2,1,0:T(8,128)S(1)} all-to-all(f32[8,8,128]{2,1,0:T(8,128)S(1)} %shard_map.76), channel_id=1, replica_groups=mesh['z'=2,'y2'=2,'y1'=2,'y0'=2,'x1'=2,'x0'=2,'zl'=4,'c'=2] {'zl','c'}, dimensions={0} | all-to-all | bytes 65536 | tf_op jit(solution)/shard_map/all_to_all | solution.py:226
  89.5 0.6 reduce_sum.9
  (15 shorter events, 0.2 us)
Async XLA Ops:
  0.0 11.6 %copy-start = (bf16[2048,176]{0,1:T(8,128)(2,1)S(1)}, bf16[2048,176]{0,1:T(8,128)(2,1)}, u32[]{:S(2)}) copy-start(bf16[2048,176]{0,1:T(8,128)(2,1)} %param.9) | copy-start | bytes 2162692
  0.0 24.9 %collective-permute-start.1 = (bf16[16,512]{1,0:T(8,128)(2,1)}, bf16[16,512]{1,0:T(8,128)(2,1)S(1)}, u32[]{:S(2)}, u32[]{:S(2)}) collective-permute-start(bf16[16,512]{1,0:T(8,128)(2,1)} %param.12), channel_id=1, source_target_pairs={{0,256},{256,0},{1,257},{257,1},{2,258},{258,2},{3,259},{259,3},{4... | collective-permute-start | bytes 49160 | tf_op jit(solution)/shard_map/ppermute | solution.py:194
  12.6 5.1 %slice-start = ((s8[5767168]{0:T(1024)(128)(4,1)}), s8[4194304]{0:T(1024)(128)(4,1)S(1)}, s32[]{:S(2)}) async-start(s8[5767168]{0:T(1024)(128)(4,1)} %bitcast.18), calls=%async_computation.2 | async-start | bytes 8388608
  12.7 5.1 %slice-start.1 = ((s8[5767168]{0:T(1024)(128)(4,1)}), s8[1572864]{0:T(1024)(128)(4,1)S(1)}, s32[]{:S(2)}) async-start(s8[5767168]{0:T(1024)(128)(4,1)} %bitcast.18), calls=%async_computation.3 | async-start | bytes 3145728
  12.7 5.1 %copy-start.1 = (bf16[1408,768]{1,0:T(8,128)(2,1)S(1)}, bf16[1408,768]{1,0:T(8,128)(2,1)}, u32[]{:S(2)}) copy-start(bf16[1408,768]{1,0:T(8,128)(2,1)} %w_ref.1) | copy-start | bytes 6488068
  12.7 5.1 %copy-start.2 = (bf16[768,64]{0,1:T(8,128)(2,1)S(1)}, bf16[768,64]{0,1:T(8,128)(2,1)}, u32[]{:S(2)}) copy-start(bf16[768,64]{0,1:T(8,128)(2,1)} %param.10) | copy-start | bytes 294916
  12.7 12.2 %collective-permute-start = (bf16[64,1024]{1,0:T(8,128)(2,1)S(1)}, bf16[64,1024]{1,0:T(8,128)(2,1)S(1)}, u32[]{:S(2)}, u32[]{:S(2)}) collective-permute-start(bf16[64,1024]{1,0:T(8,128)(2,1)S(1)} %dynamic-slice_convert_fusion), channel_id=1, source_target_pairs={{0,1},{1,0},{2,3},{3,2},{4,5},{5,4},{6,7},{7,6},{8,9},{9,8},{10,11... | collective-permute-start | bytes 393224 | tf_op jit(solution)/shard_map/ppermute | solution.py:199
  15.8 0.7 copy-start.3
  17.8 7.1 %copy-start.4 = (bf16[16,512]{1,0:T(8,128)(2,1)S(1)}, bf16[16,512]{1,0:T(8,128)(2,1)}, u32[]{:S(2)}) copy-start(bf16[16,512]{1,0:T(8,128)(2,1)} %param.12) | copy-start | bytes 49156
  25.0 11.9 %collective-permute-start.2 = (bf16[64,1024]{1,0:T(8,128)(2,1)S(1)}, bf16[64,1024]{1,0:T(8,128)(2,1)S(1)}, u32[]{:S(2)}, u32[]{:S(2)}) collective-permute-start(bf16[64,1024]{1,0:T(8,128)(2,1)S(1)} %convert_element_type.41), channel_id=1, source_target_pairs={{0,2},{2,0},{4,6},{6,4},{1,3},{3,1},{5,7},{7,5},{8,10},{10,8},{12,... | collective-permute-start | bytes 393224 | tf_op jit(solution)/shard_map/ppermute | solution.py:205
  28.1 8.8 %collective-permute-start.3 = (bf16[32,512]{1,0:T(8,128)(2,1)S(1)}, bf16[32,512]{1,0:T(8,128)(2,1)S(1)}, u32[]{:S(2)}, u32[]{:S(2)}) collective-permute-start(bf16[32,512]{1,0:T(8,128)(2,1)S(1)} %pad_maximum_fusion.3), channel_id=1, source_target_pairs={{0,128},{128,0},{1,129},{129,1},{2,130},{130,2},{3,131},{131,3},{4... | collective-permute-start | bytes 98312 | tf_op jit(solution)/shard_map/ppermute | solution.py:204
  36.9 10.6 %collective-permute-start.6 = (bf16[64,1024]{1,0:T(8,128)(2,1)S(1)}, bf16[64,1024]{1,0:T(8,128)(2,1)S(1)}, u32[]{:S(2)}, u32[]{:S(2)}) collective-permute-start(bf16[64,1024]{1,0:T(8,128)(2,1)S(1)} %fusion), channel_id=1, source_target_pairs={{0,4},{4,0},{2,6},{6,2},{1,5},{5,1},{3,7},{7,3},{8,12},{12,8},{10,... | collective-permute-start | bytes 393224 | tf_op jit(solution)/shard_map/ppermute | solution.py:211
  40.9 9.4 %collective-permute-start.4 = (bf16[64,512]{1,0:T(8,128)(2,1)S(1)}, bf16[64,512]{1,0:T(8,128)(2,1)S(1)}, u32[]{:S(2)}, u32[]{:S(2)}) collective-permute-start(bf16[64,512]{1,0:T(8,128)(2,1)S(1)} %pad_maximum_fusion.2), channel_id=1, source_target_pairs={{0,16},{16,0},{1,17},{17,1},{2,18},{18,2},{3,19},{19,3},{4,20},{20... | collective-permute-start | bytes 196616 | tf_op jit(solution)/shard_map/ppermute | solution.py:208
  47.6 7.3 %collective-permute-start.7 = (bf16[64,1024]{1,0:T(8,128)(2,1)S(1)}, bf16[64,1024]{1,0:T(8,128)(2,1)S(1)}, u32[]{:S(2)}, u32[]{:S(2)}) collective-permute-start(bf16[64,1024]{1,0:T(8,128)(2,1)S(1)} %add_convert_fusion.o1_ref), channel_id=1, source_target_pairs={{0,1},{1,0},{2,3},{3,2},{4,5},{5,4},{6,7},{7,6},{8,9},{9,8},{10,11... | collective-permute-start | bytes 393224 | tf_op jit(solution)/shard_map/ppermute | solution.py:213
  50.4 10.9 %collective-permute-start.5 = (bf16[128,512]{1,0:T(8,128)(2,1)S(1)}, bf16[128,512]{1,0:T(8,128)(2,1)S(1)}, u32[]{:S(2)}, u32[]{:S(2)}) collective-permute-start(bf16[128,512]{1,0:T(8,128)(2,1)S(1)} %pad_maximum_fusion.1), channel_id=1, source_target_pairs={{0,64},{64,0},{1,65},{65,1},{2,66},{66,2},{3,67},{67,3},{4,68},{68... | collective-permute-start | bytes 393224 | tf_op jit(solution)/shard_map/ppermute | solution.py:209
  55.8 5.6 %collective-permute-start.8 = (bf16[4,32,128]{2,1,0:T(8,128)(2,1)S(1)}, bf16[4,32,128]{2,1,0:T(8,128)(2,1)S(1)}, u32[]{:S(2)}, u32[]{:S(2)}) collective-permute-start(bf16[4,32,128]{2,1,0:T(8,128)(2,1)S(1)} %get-tuple-element.28), channel_id=1, source_target_pairs={{0,1},{1,0},{2,3},{3,2},{4,5},{5,4},{6,7},{7,6},{8,9},{9,8},{10,11... | collective-permute-start | bytes 98312 | tf_op jit(solution)/shard_map/ppermute | solution.py:216
  62.5 16.6 %all-to-all-start = ((bf16[4,256,512]{2,1,0:T(8,128)(2,1)}), bf16[4,256,512]{2,1,0:T(8,128)(2,1)S(1)}, u32[]{:S(2)}, u32[]{:S(2)}) async-start(bf16[4,256,512]{2,1,0:T(8,128)(2,1)} %broadcast_in_dim.2), calls=%async_computation | async-start | bytes 2097152 | tf_op jit(solution)/shard_map/all_to_all | solution.py:182
  66.0 4.5 %collective-permute-start.9 = (bf16[2,32,128]{2,1,0:T(8,128)(2,1)S(1)}, bf16[2,32,128]{2,1,0:T(8,128)(2,1)S(1)}, u32[]{:S(2)}, u32[]{:S(2)}) collective-permute-start(bf16[2,32,128]{2,1,0:T(8,128)(2,1)S(1)} %fusion.1), channel_id=1, source_target_pairs={{0,2},{2,0},{4,6},{6,4},{1,3},{3,1},{5,7},{7,5},{8,10},{10,8},{12,... | collective-permute-start | bytes 49160 | tf_op jit(solution)/shard_map/ppermute | solution.py:222
  70.5 5.6 %collective-permute-start.10 = (bf16[32,128]{1,0:T(8,128)(2,1)S(1)}, bf16[32,128]{1,0:T(8,128)(2,1)S(1)}, u32[]{:S(2)}, u32[]{:S(2)}) collective-permute-start(bf16[32,128]{1,0:T(8,128)(2,1)S(1)} %fusion.2), channel_id=1, source_target_pairs={{0,4},{4,0},{2,6},{6,2},{1,5},{5,1},{3,7},{7,3},{8,12},{12,8},{10,... | collective-permute-start | bytes 24584 | tf_op jit(solution)/shard_map/ppermute | solution.py:225

commit v3 on v1

--- a/solution.py
+++ b/solution.py
@@ -14,7 +14,7 @@
 DP = PARTS[:6]
 TENSOR = PARTS[6:]
 SWAP = [(0, 1), (1, 0)]
-ORDER = ("x0", "y0", "x1", "y1", "y2", "z")
+ORDER = ("y0", "x0", "x1", "y1", "y2", "z")
 VMEM = pl.BlockSpec(memory_space=pltpu.VMEM)
 ANY = pl.BlockSpec(memory_space=pl.ANY)
 SMEM = pl.BlockSpec(memory_space=pltpu.SMEM)
@@ -130,7 +130,7 @@
     )(scene, near(o1), near(o2), near(i))
 
 
-def score_kernel(f_ref, q1_ref, q2_ref, out_ref, own, turned, feat):
+def score_kernel(f_ref, q_ref, out_ref, own, turned, feat):
     group = lax.axis_index("z") * 4 + lax.axis_index("y2") * 2
     total = f_ref[0].astype(f32)
     for t in range(1, 8):
@@ -144,7 +144,6 @@
         feat[0:4, cols] = jnp.where(low, own[even, :], turned[odd, :])
         feat[4:8, cols] = jnp.where(low, turned[even, :], own[odd, :])
     f = feat[...].astype(bf16)
-    lanes = lax.broadcasted_iota(jnp.int32, (8, 128), 1)
     for t in range(8):
         rows = []
         for b in range(8):
@@ -152,21 +151,17 @@
             row = 0
             for axis in ORDER:
                 row = 2 * row + (bits[axis] > 0)
-            ref, row = (q1_ref, row) if row < 32 else (q2_ref, row - 32)
-            rows.append(ref[16 * row : 16 * row + 16, :])
+            rows.append(q_ref[16 * row : 16 * row + 16, :])
         x = lax.dot_general(
             f, jnp.concatenate(rows, axis=0), (((1,), (1,)), ((), ())), preferred_element_type=f32
         )
-        for axis, width in (("y0", 64), ("x0", 16)):
-            other = jnp.where((lanes & width) == 0, pltpu.roll(x, 128 - width, 1), pltpu.roll(x, width, 1))
-            x = jnp.where(lax.axis_index(axis) == 1, other, x)
         out_ref[t ^ group] = x
 
 
-def partial_scores(f, q1, q2):
+def partial_scores(f, q):
     return pl.pallas_call(
         score_kernel,
-        in_specs=[VMEM] * 3,
+        in_specs=[VMEM] * 2,
         out_specs=VMEM,
         out_shape=jax.ShapeDtypeStruct((8, 8, 128), f32),
         scratch_shapes=[
@@ -176,7 +171,7 @@
         ],
         compiler_params=pltpu.CompilerParams(vmem_limit_bytes=8 * 2**20),
         cost_estimate=pl.CostEstimate(flops=2 * 256 * 512 * 1024, bytes_accessed=2**20, transcendentals=0),
-    )(f, q1, q2)
+    )(f, q)
 
 
 def gather(x, axes):
@@ -209,12 +204,11 @@
     q = jnp.concatenate([q, lax.ppermute(q, "y2", SWAP)], axis=0)
     q = gather(q, ("x1", "y1"))
     q, o1, o2 = tie((q, o1, o2))
-    q = jnp.concatenate([q, lax.ppermute(q, "y0", SWAP)], axis=0)
+    q = gather(q, ("y0", "x0"))
     f = features(scene, o1, o2, i)
     q, f = tie((q, f))
-    q2 = lax.ppermute(q, "x0", SWAP)
     f = lax.all_to_all(f, TENSOR, 0, 0)
-    scores = partial_scores(near(f), near(q), near(q2))
+    scores = partial_scores(near(f), near(q))
     return jnp.sum(lax.all_to_all(scores, TENSOR, 0, 0), axis=0)
 
 

time: 87.7 us -> 91 us (1.038); the launches traced: 86.2 us -> 90.5 us
  waiting for transfers between devices: 10.7 us -> 19.8 us
  blocking collectives: 21.3 us -> 17.1 us
    all_to_all x1 -> x2, waiting for transfers between devices: 3.46 us -> 16.8 us  [gather(): lax.all_to_all(jnp.broadcast_to(x[None], (count,) + x.shape), axes, 0, 0)]
    ppermute x1, starting transfers between devices: 5.4 us -> 11.6 us  [local(): q = jnp.concatenate([queries, lax.ppermute(queries, 'z', SWAP)], axis=0)]
    ppermute x1, starting transfers between devices: 9.05 us -> 3.13 us  [local(): o = o1 + lax.ppermute(o2.astype(bf16), 'c', SWAP).astype(f32)]
    ppermute x2 -> x0, waiting for transfers between devices: 4.27 us -> none  [the longest x1 4.26 us: local(): q = jnp.concatenate([q, lax.ppermute(q, 'y0', SWAP)], axis=0)]
    ppermute x2 -> x0, starting transfers between devices: 4.19 us -> none  [the longest x1 2.28 us: local(): q2 = lax.ppermute(q, 'x0', SWAP)]
    all_to_all x1 -> x2, starting transfers between devices: 4.23 us -> 7.76 us  [gather(): lax.all_to_all(jnp.broadcast_to(x[None], (count,) + x.shape), axes, 0, 0)]
    all_to_all x1, blocking collectives: 11.8 us -> 8.95 us  [local(): f = lax.all_to_all(f, TENSOR, 0, 0)]
    all_to_all x1, blocking collectives: 9.53 us -> 8.19 us  [local(): return jnp.sum(lax.all_to_all(scores, TENSOR, 0, 0), axis=0)]
  transfers between devices with their start and end apart: 9 -> 8, of which waited for: 4 -> 4; matrix products, arithmetic and copies ran while one was open for 1% -> 2% of each run, Pallas kernels for 11% -> 10%
where the time goes in v3:
time: 91 us; the launch traced here: 90.5 us
  starting transfers between devices  39.4 us (43%)
  waiting for transfers between devices  19.8 us (22%)
  blocking collectives  17.1 us (19%)
  Pallas kernels  9.62 us (11%)
  local copies, waits for them, and re-layouts  2.48 us (3%)
  matrix products  1.01 us (1%)
    all_to_all x2, waiting for transfers between devices, gather(): lax.all_to_all(jnp.broadcast_to(x[None], (count,) + x.shape), axes, 0, 0)  16.8 us
    ppermute x1, starting transfers between devices, local(): q = jnp.concatenate([queries, lax.ppermute(queries, 'z', SWAP)], axis=0)  11.6 us
    all_to_all x1, blocking collectives, local(): f = lax.all_to_all(f, TENSOR, 0, 0)  8.95 us
    all_to_all x1, blocking collectives, local(): return jnp.sum(lax.all_to_all(scores, TENSOR, 0, 0), axis=0)  8.19 us
    all_to_all x2, starting transfers between devices, gather(): lax.all_to_all(jnp.broadcast_to(x[None], (count,) + x.shape), axes, 0, 0)  7.76 us
    ppermute x1, starting transfers between devices, local(): q = jnp.concatenate([q, lax.ppermute(q, 'y2', SWAP)], axis=0)  7.45 us
    pallas_call x1, Pallas kernels, in_project(): pl.pallas_call(in_kernel, in_specs=[VMEM] * 3, out_specs=VMEM, out_shape=...  7.02 us
    ppermute x1, starting transfers between devices, local(): o = o + lax.ppermute(o.astype(bf16), 'zl', FAR).astype(f32)  4.01 us
  transfers between devices with their start and end apart: 8, of which 4 were waited for; matrix products, arithmetic and copies ran while one was open for 2% of the time, Pallas kernels for 10%

profile of v3, /device:TPU:1, one launch (start us, length us, event | category | flops | bytes accessed | tf_op | source)
XLA Modules:
  0.0 90.5 jit_solution(5585262458238213297)
XLA Ops:
  0.0 0.0 copy-start
  0.0 11.6 %collective-permute-start.1 = (bf16[16,512]{1,0:T(8,128)(2,1)}, bf16[16,512]{1,0:T(8,128)(2,1)S(1)}, u32[]{:S(2)}, u32[]{:S(2)}) collective-permute-start(bf16[16,512]{1,0:T(8,128)(2,1)} %param.12), channel_id=1, source_target_pairs={{0,256},{256,0},{1,257},{257,1},{2,258},{258,2},{3,259},{259,3},{4... | collective-permute-start | bytes 49160 | tf_op jit(solution)/shard_map/ppermute | solution.py:191
  11.6 0.0 copy-done
  11.6 1.0 %fusion.1 = f32[64,2048]{1,0:T(8,128)S(1)} fusion(bf16[176,64]{0,1:T(8,128)(2,1)} %param.11, bf16[2048,176]{0,1:T(8,128)(2,1)S(1)} %copy-done), kind=kOutput, calls=%fused_computation.7 | convolution fusion | flops 46137344 | bytes 1267712 | tf_op jit(solution)/shard_map/dot_general | solution.py:192
  12.6 0.0 slice-start
  12.7 0.0 slice-start.1
  12.7 0.0 copy-start.1
  12.7 0.0 copy-start.2
  12.7 3.1 %collective-permute-start = (bf16[64,1024]{1,0:T(8,128)(2,1)S(1)}, bf16[64,1024]{1,0:T(8,128)(2,1)S(1)}, u32[]{:S(2)}, u32[]{:S(2)}) collective-permute-start(bf16[64,1024]{1,0:T(8,128)(2,1)S(1)} %dynamic-slice_convert_fusion), channel_id=1, source_target_pairs={{0,1},{1,0},{2,3},{3,2},{4,5},{5,4},{6,7},{7,6},{8,9},{9,8},{10,11... | collective-permute-start | bytes 393224 | tf_op jit(solution)/shard_map/ppermute | solution.py:196
  15.8 0.0 copy-start.3
  15.9 0.6 copy-done.3
  16.5 1.3 %shard_map.73.scene_ref = s32[16]{0:T(128)S(1)} custom-call(s32[1,8]{1,0:T(1,128)S(1)} %copy-done.3), custom_call_target="tpu_custom_call" | custom-call | flops 20000000000 | bytes 64 | tf_op jit(solution)/shard_map/pallas_call | solution.py:59
  17.8 0.0 slice-done
  17.8 0.0 slice-done.1
  17.8 0.0 copy-done.1
  17.8 0.0 copy-done.2
  17.8 0.0 copy-start.4
  17.8 7.0 %shard_map.74.i_ref = bf16[2,64,1024]{2,1,0:T(8,128)(2,1)S(1)} custom-call(bf16[2048,1408]{1,0:T(8,128)(2,1)S(1)} %bitcast.7, bf16[1408,768]{1,0:T(8,128)(2,1)S(1)} %copy-done.1, bf16[64,768]{1,0:T(8,128)(2,1)S(1)} %bitcast.8), custom_call_target="tpu_custom_call" | custom-call | flops 5234491392 | bytes 7929856 | tf_op jit(solution)/shard_map/pallas_call | solution.py:88
  24.9 0.0 collective-permute-done.1
  24.9 0.0 copy-done.4
  24.9 0.0 collective-permute-done
  25.0 3.1 %collective-permute-start.3 = (bf16[64,1024]{1,0:T(8,128)(2,1)S(1)}, bf16[64,1024]{1,0:T(8,128)(2,1)S(1)}, u32[]{:S(2)}, u32[]{:S(2)}) collective-permute-start(bf16[64,1024]{1,0:T(8,128)(2,1)S(1)} %convert_element_type.23), channel_id=1, source_target_pairs={{0,2},{2,0},{4,6},{6,4},{1,3},{3,1},{5,7},{7,5},{8,10},{10,8},{12,... | collective-permute-start | bytes 393224 | tf_op jit(solution)/shard_map/ppermute | solution.py:200
  28.1 7.5 %collective-permute-start.2 = (bf16[32,512]{1,0:T(8,128)(2,1)S(1)}, bf16[32,512]{1,0:T(8,128)(2,1)S(1)}, u32[]{:S(2)}, u32[]{:S(2)}) collective-permute-start(bf16[32,512]{1,0:T(8,128)(2,1)S(1)} %pad_maximum_fusion.1), channel_id=1, source_target_pairs={{0,128},{128,0},{1,129},{129,1},{2,130},{130,2},{3,131},{131,3},{4... | collective-permute-start | bytes 98312 | tf_op jit(solution)/shard_map/ppermute | solution.py:204
  35.5 0.0 collective-permute-done.3
  35.6 4.0 %collective-permute-start.4 = (bf16[64,1024]{1,0:T(8,128)(2,1)S(1)}, bf16[64,1024]{1,0:T(8,128)(2,1)S(1)}, u32[]{:S(2)}, u32[]{:S(2)}) collective-permute-start(bf16[64,1024]{1,0:T(8,128)(2,1)S(1)} %fusion), channel_id=1, source_target_pairs={{0,4},{4,0},{2,6},{6,2},{1,5},{5,1},{3,7},{7,3},{8,12},{12,8},{10,... | collective-permute-start | bytes 393224 | tf_op jit(solution)/shard_map/ppermute | solution.py:201
  39.6 0.0 collective-permute-done.2
  39.6 0.7 broadcast_in_dim.4
  40.3 4.2 %all-to-all-start = ((bf16[4,64,512]{2,1,0:T(8,128)(2,1)}), bf16[4,64,512]{2,1,0:T(8,128)(2,1)S(1)}, u32[]{:S(2)}, u32[]{:S(2)}) async-start(bf16[4,64,512]{2,1,0:T(8,128)(2,1)} %broadcast_in_dim.4), calls=%async_computation | async-start | bytes 524288 | tf_op jit(solution)/shard_map/all_to_all | solution.py:179
  44.6 2.0 %collective-permute-done.4 = bf16[64,1024]{1,0:T(8,128)(2,1)S(1)} collective-permute-done((bf16[64,1024]{1,0:T(8,128)(2,1)S(1)}, bf16[64,1024]{1,0:T(8,128)(2,1)S(1)}, u32[]{:S(2)}, u32[]{:S(2)}) %collective-permute-start.4) | collective-permute-done | bytes 131104 | tf_op jit(solution)/shard_map/ppermute | solution.py:201
  46.6 2.4 %collective-permute-start.5 = (bf16[64,1024]{1,0:T(8,128)(2,1)S(1)}, bf16[64,1024]{1,0:T(8,128)(2,1)S(1)}, u32[]{:S(2)}, u32[]{:S(2)}) collective-permute-start(bf16[64,1024]{1,0:T(8,128)(2,1)S(1)} %add_convert_fusion.o1_ref), channel_id=1, source_target_pairs={{0,1},{1,0},{2,3},{3,2},{4,5},{5,4},{6,7},{7,6},{8,9},{9,8},{10,11... | collective-permute-start | bytes 393224 | tf_op jit(solution)/shard_map/ppermute | solution.py:203
  49.0 1.0 %collective-permute-done.5.o2_ref = bf16[64,1024]{1,0:T(8,128)(2,1)S(1)} collective-permute-done((bf16[64,1024]{1,0:T(8,128)(2,1)S(1)}, bf16[64,1024]{1,0:T(8,128)(2,1)S(1)}, u32[]{:S(2)}, u32[]{:S(2)}) %collective-permute-start.5) | collective-permute-done | bytes 131104 | tf_op jit(solution)/shard_map/ppermute | solution.py:203
  50.0 4.7 %all-to-all-done = bf16[4,64,512]{2,1,0:T(8,128)(2,1)S(1)} async-done(((bf16[4,64,512]{2,1,0:T(8,128)(2,1)}), bf16[4,64,512]{2,1,0:T(8,128)(2,1)S(1)}, u32[]{:S(2)}, u32[]{:S(2)}) %all-to-all-start) | async-done | bytes 262176 | tf_op jit(solution)/shard_map/all_to_all | solution.py:179
  54.7 1.1 %broadcast_in_dim.5 = bf16[4,256,512]{2,1,0:T(8,128)(2,1)} broadcast(bf16[256,512]{1,0:T(8,128)(2,1)S(1)} %bitcast.9), dimensions={1,2} | broadcast | bytes 1310720 | tf_op jit(solution)/shard_map/broadcast_in_dim | solution.py:179
  55.7 3.5 %all-to-all-start.1 = ((bf16[4,256,512]{2,1,0:T(8,128)(2,1)}), bf16[4,256,512]{2,1,0:T(8,128)(2,1)S(1)}, u32[]{:S(2)}, u32[]{:S(2)}) async-start(bf16[4,256,512]{2,1,0:T(8,128)(2,1)} %broadcast_in_dim.5), calls=%async_computation.1 | async-start | bytes 2097152 | tf_op jit(solution)/shard_map/all_to_all | solution.py:179
  59.3 0.9 %shard_map.75 = bf16[8,32,128]{2,1,0:T(8,128)(2,1)S(1)} custom-call(s32[16]{0:T(128)S(1)} %shard_map.73.scene_ref, bf16[64,1024]{1,0:T(8,128)(2,1)S(1)} %add_convert_fusion.o1_ref, bf16[64,1024]{1,0:T(8,128)(2,1)S(1)} %collective-permute-done.5.o2_ref, bf16[2,64,1024]{2,1,0:T(8,128)(2,1)S(1)} %shard_map.74.i_ref), custom_call_target="tpu_custom_call" | custom-call | flops 20000000000 | bytes 1048576 | tf_op jit(solution)/shard_map/pallas_call | solution.py:122
  60.2 12.1 %all-to-all-done.1 = bf16[4,256,512]{2,1,0:T(8,128)(2,1)S(1)} async-done(((bf16[4,256,512]{2,1,0:T(8,128)(2,1)}), bf16[4,256,512]{2,1,0:T(8,128)(2,1)S(1)}, u32[]{:S(2)}, u32[]{:S(2)}) %all-to-all-start.1) | async-done | bytes 1048608 | tf_op jit(solution)/shard_map/all_to_all | solution.py:179
  72.3 8.9 %all_to_all.20.f_ref = bf16[8,32,128]{2,1,0:T(8,128)(2,1)S(1)} all-to-all(bf16[8,32,128]{2,1,0:T(8,128)(2,1)S(1)} %shard_map.75), channel_id=1, replica_groups=mesh['z'=2,'y2'=2,'y1'=2,'y0'=2,'x1'=2,'x0'=2,'zl'=4,'c'=2] {'zl','c'}, dimensions={0} | all-to-all | bytes 131072 | tf_op jit(solution)/shard_map/all_to_all | solution.py:210
  81.2 0.4 shard_map.76
  81.7 8.2 %all_to_all.21 = f32[8,8,128]{2,1,0:T(8,128)S(1)} all-to-all(f32[8,8,128]{2,1,0:T(8,128)S(1)} %shard_map.76), channel_id=1, replica_groups=mesh['z'=2,'y2'=2,'y1'=2,'y0'=2,'x1'=2,'x0'=2,'zl'=4,'c'=2] {'zl','c'}, dimensions={0} | all-to-all | bytes 65536 | tf_op jit(solution)/shard_map/all_to_all | solution.py:212
  89.9 0.6 reduce_sum.9
  (8 shorter events, 0.2 us)
Async XLA Ops:
  0.0 11.6 %copy-start = (bf16[2048,176]{0,1:T(8,128)(2,1)S(1)}, bf16[2048,176]{0,1:T(8,128)(2,1)}, u32[]{:S(2)}) copy-start(bf16[2048,176]{0,1:T(8,128)(2,1)} %param.9) | copy-start | bytes 2162692
  0.0 24.9 %collective-permute-start.1 = (bf16[16,512]{1,0:T(8,128)(2,1)}, bf16[16,512]{1,0:T(8,128)(2,1)S(1)}, u32[]{:S(2)}, u32[]{:S(2)}) collective-permute-start(bf16[16,512]{1,0:T(8,128)(2,1)} %param.12), channel_id=1, source_target_pairs={{0,256},{256,0},{1,257},{257,1},{2,258},{258,2},{3,259},{259,3},{4... | collective-permute-start | bytes 49160 | tf_op jit(solution)/shard_map/ppermute | solution.py:191
  12.6 5.1 %slice-start = ((s8[5767168]{0:T(1024)(128)(4,1)}), s8[4194304]{0:T(1024)(128)(4,1)S(1)}, s32[]{:S(2)}) async-start(s8[5767168]{0:T(1024)(128)(4,1)} %bitcast.6), calls=%async_computation.4 | async-start | bytes 8388608
  12.7 5.1 %slice-start.1 = ((s8[5767168]{0:T(1024)(128)(4,1)}), s8[1572864]{0:T(1024)(128)(4,1)S(1)}, s32[]{:S(2)}) async-start(s8[5767168]{0:T(1024)(128)(4,1)} %bitcast.6), calls=%async_computation.5 | async-start | bytes 3145728
  12.7 5.1 %copy-start.1 = (bf16[1408,768]{1,0:T(8,128)(2,1)S(1)}, bf16[1408,768]{1,0:T(8,128)(2,1)}, u32[]{:S(2)}) copy-start(bf16[1408,768]{1,0:T(8,128)(2,1)} %w_ref.1) | copy-start | bytes 6488068
  12.7 5.1 %copy-start.2 = (bf16[768,64]{0,1:T(8,128)(2,1)S(1)}, bf16[768,64]{0,1:T(8,128)(2,1)}, u32[]{:S(2)}) copy-start(bf16[768,64]{0,1:T(8,128)(2,1)} %param.10) | copy-start | bytes 294916
  12.7 12.2 %collective-permute-start = (bf16[64,1024]{1,0:T(8,128)(2,1)S(1)}, bf16[64,1024]{1,0:T(8,128)(2,1)S(1)}, u32[]{:S(2)}, u32[]{:S(2)}) collective-permute-start(bf16[64,1024]{1,0:T(8,128)(2,1)S(1)} %dynamic-slice_convert_fusion), channel_id=1, source_target_pairs={{0,1},{1,0},{2,3},{3,2},{4,5},{5,4},{6,7},{7,6},{8,9},{9,8},{10,11... | collective-permute-start | bytes 393224 | tf_op jit(solution)/shard_map/ppermute | solution.py:196
  15.8 0.7 copy-start.3
  17.8 7.0 %copy-start.4 = (bf16[16,512]{1,0:T(8,128)(2,1)S(1)}, bf16[16,512]{1,0:T(8,128)(2,1)}, u32[]{:S(2)}) copy-start(bf16[16,512]{1,0:T(8,128)(2,1)} %param.12) | copy-start | bytes 49156
  25.0 10.6 %collective-permute-start.3 = (bf16[64,1024]{1,0:T(8,128)(2,1)S(1)}, bf16[64,1024]{1,0:T(8,128)(2,1)S(1)}, u32[]{:S(2)}, u32[]{:S(2)}) collective-permute-start(bf16[64,1024]{1,0:T(8,128)(2,1)S(1)} %convert_element_type.23), channel_id=1, source_target_pairs={{0,2},{2,0},{4,6},{6,4},{1,3},{3,1},{5,7},{7,5},{8,10},{10,8},{12,... | collective-permute-start | bytes 393224 | tf_op jit(solution)/shard_map/ppermute | solution.py:200
  28.1 11.5 %collective-permute-start.2 = (bf16[32,512]{1,0:T(8,128)(2,1)S(1)}, bf16[32,512]{1,0:T(8,128)(2,1)S(1)}, u32[]{:S(2)}, u32[]{:S(2)}) collective-permute-start(bf16[32,512]{1,0:T(8,128)(2,1)S(1)} %pad_maximum_fusion.1), channel_id=1, source_target_pairs={{0,128},{128,0},{1,129},{129,1},{2,130},{130,2},{3,131},{131,3},{4... | collective-permute-start | bytes 98312 | tf_op jit(solution)/shard_map/ppermute | solution.py:204
  35.6 11.0 %collective-permute-start.4 = (bf16[64,1024]{1,0:T(8,128)(2,1)S(1)}, bf16[64,1024]{1,0:T(8,128)(2,1)S(1)}, u32[]{:S(2)}, u32[]{:S(2)}) collective-permute-start(bf16[64,1024]{1,0:T(8,128)(2,1)S(1)} %fusion), channel_id=1, source_target_pairs={{0,4},{4,0},{2,6},{6,2},{1,5},{5,1},{3,7},{7,3},{8,12},{12,8},{10,... | collective-permute-start | bytes 393224 | tf_op jit(solution)/shard_map/ppermute | solution.py:201
  40.3 14.3 %all-to-all-start = ((bf16[4,64,512]{2,1,0:T(8,128)(2,1)}), bf16[4,64,512]{2,1,0:T(8,128)(2,1)S(1)}, u32[]{:S(2)}, u32[]{:S(2)}) async-start(bf16[4,64,512]{2,1,0:T(8,128)(2,1)} %broadcast_in_dim.4), calls=%async_computation | async-start | bytes 524288 | tf_op jit(solution)/shard_map/all_to_all | solution.py:179
  46.6 3.4 %collective-permute-start.5 = (bf16[64,1024]{1,0:T(8,128)(2,1)S(1)}, bf16[64,1024]{1,0:T(8,128)(2,1)S(1)}, u32[]{:S(2)}, u32[]{:S(2)}) collective-permute-start(bf16[64,1024]{1,0:T(8,128)(2,1)S(1)} %add_convert_fusion.o1_ref), channel_id=1, source_target_pairs={{0,1},{1,0},{2,3},{3,2},{4,5},{5,4},{6,7},{7,6},{8,9},{9,8},{10,11... | collective-permute-start | bytes 393224 | tf_op jit(solution)/shard_map/ppermute | solution.py:203
  55.7 16.6 %all-to-all-start.1 = ((bf16[4,256,512]{2,1,0:T(8,128)(2,1)}), bf16[4,256,512]{2,1,0:T(8,128)(2,1)S(1)}, u32[]{:S(2)}, u32[]{:S(2)}) async-start(bf16[4,256,512]{2,1,0:T(8,128)(2,1)} %broadcast_in_dim.5), calls=%async_computation.1 | async-start | bytes 2097152 | tf_op jit(solution)/shard_map/all_to_all | solution.py:179

commit v4 on v1

--- a/solution.py
+++ b/solution.py
@@ -43,27 +43,41 @@
     return pltpu.with_memory_space_constraint(x, pltpu.VMEM)
 
 
-def scene_kernel(len_ref, out_ref):
+def scene_kernel(zero_ref, len_ref, out_ref):
     ends, end = [], 0
     for s in range(8):
         end = end + len_ref[0, s]
         ends.append(end)
     for block in range(16):
-        scene = 0
+        scene = zero_ref[0]
         for s in range(7):
             scene = scene + (block >= ends[s]).astype(jnp.int32)
         out_ref[block] = scene
 
 
-def scene_of_block(lengths):
+def scene_of_block(zero, lengths):
     return pl.pallas_call(
         scene_kernel,
-        in_specs=[SMEM],
+        in_specs=[SMEM, SMEM],
         out_specs=SMEM,
         out_shape=jax.ShapeDtypeStruct((16,), jnp.int32),
         compiler_params=pltpu.CompilerParams(vmem_limit_bytes=2**20),
+        cost_estimate=pl.CostEstimate(flops=10**6, bytes_accessed=64, transcendentals=0),
+    )(zero, lengths)
+
+
+def mark_kernel(out_ref):
+    out_ref[0] = 0
+
+
+def mark():
+    return pl.pallas_call(
+        mark_kernel,
+        out_specs=SMEM,
+        out_shape=jax.ShapeDtypeStruct((1,), jnp.int32),
+        compiler_params=pltpu.CompilerParams(vmem_limit_bytes=2**20),
         cost_estimate=pl.CostEstimate(flops=20 * 10**9, bytes_accessed=64, transcendentals=0),
-    )(lengths)
+    )()
 
 
 def in_kernel(x_ref, w_ref, p_ref, o_ref):
@@ -192,7 +206,7 @@
 
 def local(inputs, up_weight, out_grad, proj_in, proj_out, queries, lengths):
     core = lax.axis_index("c")
-    scene, p = tie((scene_of_block(lengths), proj_in.T))
+    zero, p = tie((mark(), proj_in.T))
     q = jnp.concatenate([queries, lax.ppermute(queries, "z", SWAP)], axis=0)
     o = lax.dot_general(proj_out, out_grad, (((0,), (1,)), ((), ())), preferred_element_type=f32)
     half = o.shape[1] // 2
@@ -201,7 +215,8 @@
     o = o1 + lax.ppermute(o2.astype(bf16), "c", SWAP).astype(f32)
     i = in_project(inputs, up_weight, p)
 
-    o, q, i = tie((o, q, i))
+    o, q, i, lengths = tie((o, q, i, lengths))
+    scene = scene_of_block(zero, lengths)
     o = o + lax.ppermute(o.astype(bf16), "zl", NEAR).astype(f32)
     o = o + lax.ppermute(o.astype(bf16), "zl", FAR).astype(f32)
     o1 = o.astype(bf16)

time: 87.7 us -> 86.3 us (0.984)
  waiting for transfers between devices: 10.7 us -> 8.78 us
  Pallas kernels: 9.77 us -> 11 us
    pallas_call x1 -> x2, Pallas kernels: 1.26 us -> 2.43 us  [the longest x1 1.91 us: scene_of_block(): pl.pallas_call(scene_kernel, in_specs=[SMEM, SMEM], out_specs=SMEM, out_s...]
    ppermute x1, waiting for transfers between devices: 0.96 us -> 0.01 us  [local(): o2 = lax.ppermute(o1, 'c', SWAP)]
    all_to_all x1, waiting for transfers between devices: 3.46 us -> 2.5 us  [gather(): lax.all_to_all(jnp.broadcast_to(x[None], (count,) + x.shape), axes, 0, 0)]
  transfers between devices with their start and end apart: 9 -> 9, of which waited for: 4 -> 3; matrix products, arithmetic and copies ran while one was open for 1% -> 1% of each run, Pallas kernels for 11% -> 12%
where the time goes in v4:
time: 86.3 us; the launch traced here: 84.8 us
  starting transfers between devices  39.8 us (46%)
  blocking collectives  21.3 us (25%)
  Pallas kernels  11 us (13%)
  waiting for transfers between devices  8.78 us (10%)
  local copies, waits for them, and re-layouts  1.89 us (2%)
  matrix products  1 us (1%)
    all_to_all x1, blocking collectives, local(): f = lax.all_to_all(f, TENSOR, 0, 0)  11.8 us
    all_to_all x1, blocking collectives, local(): return jnp.sum(lax.all_to_all(scores, TENSOR, 0, 0), axis=0)  9.53 us
    ppermute x1, starting transfers between devices, local(): o = o1 + lax.ppermute(o2.astype(bf16), 'c', SWAP).astype(f32)  9.05 us
    ppermute x1, starting transfers between devices, local(): q = jnp.concatenate([q, lax.ppermute(q, 'y2', SWAP)], axis=0)  7.46 us
    pallas_call x1, Pallas kernels, in_project(): pl.pallas_call(in_kernel, in_specs=[VMEM] * 3, out_specs=VMEM, out_shape=...  7.03 us
    ppermute x1, starting transfers between devices, local(): q = jnp.concatenate([queries, lax.ppermute(queries, 'z', SWAP)], axis=0)  5.4 us
    ppermute x1, waiting for transfers between devices, local(): q = jnp.concatenate([q, lax.ppermute(q, 'y0', SWAP)], axis=0)  4.26 us
    all_to_all x1, starting transfers between devices, gather(): lax.all_to_all(jnp.broadcast_to(x[None], (count,) + x.shape), axes, 0, 0)  4.25 us
  transfers between devices with their start and end apart: 9, of which 3 were waited for; matrix products, arithmetic and copies ran while one was open for 1% of the time, Pallas kernels for 12%

profile of v4, /device:TPU:1, one launch (start us, length us, event | category | flops | bytes accessed | tf_op | source)
XLA Modules:
  0.0 84.8 jit_solution(7032270673513301086)
XLA Ops:
  0.0 0.0 copy-start
  0.0 1.1 %copy-done = bf16[2048,176]{0,1:T(8,128)(2,1)S(1)} copy-done((bf16[2048,176]{0,1:T(8,128)(2,1)S(1)}, bf16[2048,176]{0,1:T(8,128)(2,1)}, u32[]{:S(2)}) %copy-start) | copy-done | bytes 720920
  1.1 1.0 %fusion.1 = f32[64,2048]{1,0:T(8,128)S(1)} fusion(bf16[176,64]{0,1:T(8,128)(2,1)} %param.11, bf16[2048,176]{0,1:T(8,128)(2,1)S(1)} %copy-done), kind=kOutput, calls=%fused_computation.8 | convolution fusion | flops 46137344 | bytes 1267712 | tf_op jit(solution)/shard_map/dot_general | solution.py:211
  2.1 0.0 slice-start
  2.2 0.0 slice-start.1
  2.2 0.0 copy-start.1
  2.2 0.0 copy-start.2
  2.2 9.1 %collective-permute-start = (bf16[64,1024]{1,0:T(8,128)(2,1)S(1)}, bf16[64,1024]{1,0:T(8,128)(2,1)S(1)}, u32[]{:S(2)}, u32[]{:S(2)}) collective-permute-start(bf16[64,1024]{1,0:T(8,128)(2,1)S(1)} %dynamic-slice_convert_fusion), channel_id=1, source_target_pairs={{0,1},{1,0},{2,3},{3,2},{4,5},{5,4},{6,7},{7,6},{8,9},{9,8},{10,11... | collective-permute-start | bytes 393224 | tf_op jit(solution)/shard_map/ppermute | solution.py:215
  11.3 5.4 %collective-permute-start.1 = (bf16[16,512]{1,0:T(8,128)(2,1)}, bf16[16,512]{1,0:T(8,128)(2,1)S(1)}, u32[]{:S(2)}, u32[]{:S(2)}) collective-permute-start(bf16[16,512]{1,0:T(8,128)(2,1)} %param.12), channel_id=1, source_target_pairs={{0,256},{256,0},{1,257},{257,1},{2,258},{258,2},{3,259},{259,3},{4... | collective-permute-start | bytes 49160 | tf_op jit(solution)/shard_map/ppermute | solution.py:210
  16.7 0.5 shard_map.73.zero_ref
  17.2 0.0 slice-done
  17.2 0.0 slice-done.1
  17.2 0.0 copy-done.1
  17.2 0.0 copy-done.2
  17.2 0.0 copy-start.4
  17.3 0.0 copy-start.3
  17.3 7.0 %shard_map.74.i_ref = bf16[2,64,1024]{2,1,0:T(8,128)(2,1)S(1)} custom-call(bf16[2048,1408]{1,0:T(8,128)(2,1)S(1)} %bitcast.5, bf16[1408,768]{1,0:T(8,128)(2,1)S(1)} %copy-done.1, bf16[64,768]{1,0:T(8,128)(2,1)S(1)} %bitcast.6), custom_call_target="tpu_custom_call" | custom-call | flops 5234491392 | bytes 7929856 | tf_op jit(solution)/shard_map/pallas_call | solution.py:102
  24.3 0.0 collective-permute-done.1
  24.3 0.0 copy-done.4
  24.3 0.0 collective-permute-done
  24.4 3.1 %collective-permute-start.3 = (bf16[64,1024]{1,0:T(8,128)(2,1)S(1)}, bf16[64,1024]{1,0:T(8,128)(2,1)S(1)}, u32[]{:S(2)}, u32[]{:S(2)}) collective-permute-start(bf16[64,1024]{1,0:T(8,128)(2,1)S(1)} %convert_element_type.23), channel_id=1, source_target_pairs={{0,2},{2,0},{4,6},{6,4},{1,3},{3,1},{5,7},{7,5},{8,10},{10,8},{12,... | collective-permute-start | bytes 393224 | tf_op jit(solution)/shard_map/ppermute | solution.py:220
  27.5 7.5 %collective-permute-start.2 = (bf16[32,512]{1,0:T(8,128)(2,1)S(1)}, bf16[32,512]{1,0:T(8,128)(2,1)S(1)}, u32[]{:S(2)}, u32[]{:S(2)}) collective-permute-start(bf16[32,512]{1,0:T(8,128)(2,1)S(1)} %pad_maximum_fusion.2), channel_id=1, source_target_pairs={{0,128},{128,0},{1,129},{129,1},{2,130},{130,2},{3,131},{131,3},{4... | collective-permute-start | bytes 98312 | tf_op jit(solution)/shard_map/ppermute | solution.py:224
  35.0 0.0 collective-permute-done.3
  35.0 4.0 %collective-permute-start.4 = (bf16[64,1024]{1,0:T(8,128)(2,1)S(1)}, bf16[64,1024]{1,0:T(8,128)(2,1)S(1)}, u32[]{:S(2)}, u32[]{:S(2)}) collective-permute-start(bf16[64,1024]{1,0:T(8,128)(2,1)S(1)} %fusion), channel_id=1, source_target_pairs={{0,4},{4,0},{2,6},{6,2},{1,5},{5,1},{3,7},{7,3},{8,12},{12,8},{10,... | collective-permute-start | bytes 393224 | tf_op jit(solution)/shard_map/ppermute | solution.py:221
  39.0 0.0 collective-permute-done.2
  39.1 0.7 broadcast_in_dim.2
  39.8 4.3 %all-to-all-start = ((bf16[4,64,512]{2,1,0:T(8,128)(2,1)}), bf16[4,64,512]{2,1,0:T(8,128)(2,1)S(1)}, u32[]{:S(2)}, u32[]{:S(2)}) async-start(bf16[4,64,512]{2,1,0:T(8,128)(2,1)} %broadcast_in_dim.2), calls=%async_computation | async-start | bytes 524288 | tf_op jit(solution)/shard_map/all_to_all | solution.py:198
  44.0 2.0 %collective-permute-done.4 = bf16[64,1024]{1,0:T(8,128)(2,1)S(1)} collective-permute-done((bf16[64,1024]{1,0:T(8,128)(2,1)S(1)}, bf16[64,1024]{1,0:T(8,128)(2,1)S(1)}, u32[]{:S(2)}, u32[]{:S(2)}) %collective-permute-start.4) | collective-permute-done | bytes 131104 | tf_op jit(solution)/shard_map/ppermute | solution.py:221
  46.1 2.4 %collective-permute-start.5 = (bf16[64,1024]{1,0:T(8,128)(2,1)S(1)}, bf16[64,1024]{1,0:T(8,128)(2,1)S(1)}, u32[]{:S(2)}, u32[]{:S(2)}) collective-permute-start(bf16[64,1024]{1,0:T(8,128)(2,1)S(1)} %add_convert_fusion.o1_ref), channel_id=1, source_target_pairs={{0,1},{1,0},{2,3},{3,2},{4,5},{5,4},{6,7},{7,6},{8,9},{9,8},{10,11... | collective-permute-start | bytes 393224 | tf_op jit(solution)/shard_map/ppermute | solution.py:223
  48.5 0.0 copy-done.3
  48.5 1.9 %shard_map.75.scene_ref = s32[16]{0:T(128)S(1)} custom-call(s32[1]{0:T(128)} %shard_map.73.zero_ref, s32[1,8]{1,0:T(1,128)S(1)} %copy-done.3), custom_call_target="tpu_custom_call" | custom-call | flops 1000000 | bytes 64 | tf_op jit(solution)/shard_map/pallas_call | solution.py:59
  50.4 0.0 collective-permute-done.5.o2_ref
  50.4 2.5 %all-to-all-done = bf16[4,64,512]{2,1,0:T(8,128)(2,1)S(1)} async-done(((bf16[4,64,512]{2,1,0:T(8,128)(2,1)}), bf16[4,64,512]{2,1,0:T(8,128)(2,1)S(1)}, u32[]{:S(2)}, u32[]{:S(2)}) %all-to-all-start) | async-done | bytes 262176 | tf_op jit(solution)/shard_map/all_to_all | solution.py:198
  52.9 1.9 %collective-permute-start.6 = (bf16[256,512]{1,0:T(8,128)(2,1)S(1)}, bf16[256,512]{1,0:T(8,128)(2,1)S(1)}, u32[]{:S(2)}, u32[]{:S(2)}) collective-permute-start(bf16[256,512]{1,0:T(8,128)(2,1)S(1)} %bitcast.7), channel_id=1, source_target_pairs={{0,32},{32,0},{1,33},{33,1},{2,34},{34,2},{3,35},{35,3},{4,36},{36... | collective-permute-start | bytes 786440 | tf_op jit(solution)/shard_map/ppermute | solution.py:227
  54.8 0.9 %shard_map.76 = bf16[8,32,128]{2,1,0:T(8,128)(2,1)S(1)} custom-call(s32[16]{0:T(128)S(1)} %shard_map.75.scene_ref, bf16[64,1024]{1,0:T(8,128)(2,1)S(1)} %add_convert_fusion.o1_ref, bf16[64,1024]{1,0:T(8,128)(2,1)S(1)} %collective-permute-done.5.o2_ref, bf16[2,64,1024]{2,1,0:T(8,128)(2,1)S(1)} %shard_map.74.i_ref), custom_call_target="tpu_custom_call" | custom-call | flops 20000000000 | bytes 1048576 | tf_op jit(solution)/shard_map/pallas_call | solution.py:136
  55.8 4.3 %collective-permute-done.6 = bf16[256,512]{1,0:T(8,128)(2,1)S(1)} collective-permute-done((bf16[256,512]{1,0:T(8,128)(2,1)S(1)}, bf16[256,512]{1,0:T(8,128)(2,1)S(1)}, u32[]{:S(2)}, u32[]{:S(2)}) %collective-permute-start.6) | collective-permute-done | bytes 262176 | tf_op jit(solution)/shard_map/ppermute | solution.py:227
  60.1 2.3 %collective-permute-start.7 = (bf16[512,512]{1,0:T(8,128)(2,1)S(1)}, bf16[512,512]{1,0:T(8,128)(2,1)S(1)}, u32[]{:S(2)}, u32[]{:S(2)}) collective-permute-start(bf16[512,512]{1,0:T(8,128)(2,1)S(1)} %pad_maximum_fusion.q1_ref), channel_id=1, source_target_pairs={{0,8},{8,0},{1,9},{9,1},{2,10},{10,2},{3,11},{11,3},{4,12},{12,4},... | collective-permute-start | bytes 1572872 | tf_op jit(solution)/shard_map/ppermute | solution.py:230
  62.3 11.8 %all_to_all.15.f_ref = bf16[8,32,128]{2,1,0:T(8,128)(2,1)S(1)} all-to-all(bf16[8,32,128]{2,1,0:T(8,128)(2,1)S(1)} %shard_map.76), channel_id=1, replica_groups=mesh['z'=2,'y2'=2,'y1'=2,'y0'=2,'x1'=2,'x0'=2,'zl'=4,'c'=2] {'zl','c'}, dimensions={0} | all-to-all | bytes 131072 | tf_op jit(solution)/shard_map/all_to_all | solution.py:231
  74.1 0.0 collective-permute-done.7.q2_ref
  74.1 0.6 shard_map.77
  74.7 9.5 %all_to_all.16 = f32[8,8,128]{2,1,0:T(8,128)S(1)} all-to-all(f32[8,8,128]{2,1,0:T(8,128)S(1)} %shard_map.77), channel_id=1, replica_groups=mesh['z'=2,'y2'=2,'y1'=2,'y0'=2,'x1'=2,'x0'=2,'zl'=4,'c'=2] {'zl','c'}, dimensions={0} | all-to-all | bytes 65536 | tf_op jit(solution)/shard_map/all_to_all | solution.py:233
  84.2 0.6 reduce_sum.9
  (9 shorter events, 0.2 us)
Async XLA Ops:
  0.0 1.1 %copy-start = (bf16[2048,176]{0,1:T(8,128)(2,1)S(1)}, bf16[2048,176]{0,1:T(8,128)(2,1)}, u32[]{:S(2)}) copy-start(bf16[2048,176]{0,1:T(8,128)(2,1)} %param.9) | copy-start | bytes 2162692
  2.1 15.1 %slice-start = ((s8[5767168]{0:T(1024)(128)(4,1)}), s8[4194304]{0:T(1024)(128)(4,1)S(1)}, s32[]{:S(2)}) async-start(s8[5767168]{0:T(1024)(128)(4,1)} %bitcast.4), calls=%async_computation.3 | async-start | bytes 8388608
  2.2 15.0 %slice-start.1 = ((s8[5767168]{0:T(1024)(128)(4,1)}), s8[1572864]{0:T(1024)(128)(4,1)S(1)}, s32[]{:S(2)}) async-start(s8[5767168]{0:T(1024)(128)(4,1)} %bitcast.4), calls=%async_computation.4 | async-start | bytes 3145728
  2.2 15.0 %copy-start.1 = (bf16[1408,768]{1,0:T(8,128)(2,1)S(1)}, bf16[1408,768]{1,0:T(8,128)(2,1)}, u32[]{:S(2)}) copy-start(bf16[1408,768]{1,0:T(8,128)(2,1)} %w_ref.1) | copy-start | bytes 6488068
  2.2 15.0 %copy-start.2 = (bf16[768,64]{0,1:T(8,128)(2,1)S(1)}, bf16[768,64]{0,1:T(8,128)(2,1)}, u32[]{:S(2)}) copy-start(bf16[768,64]{0,1:T(8,128)(2,1)} %param.10) | copy-start | bytes 294916
  2.2 22.1 %collective-permute-start = (bf16[64,1024]{1,0:T(8,128)(2,1)S(1)}, bf16[64,1024]{1,0:T(8,128)(2,1)S(1)}, u32[]{:S(2)}, u32[]{:S(2)}) collective-permute-start(bf16[64,1024]{1,0:T(8,128)(2,1)S(1)} %dynamic-slice_convert_fusion), channel_id=1, source_target_pairs={{0,1},{1,0},{2,3},{3,2},{4,5},{5,4},{6,7},{7,6},{8,9},{9,8},{10,11... | collective-permute-start | bytes 393224 | tf_op jit(solution)/shard_map/ppermute | solution.py:215
  11.3 13.0 %collective-permute-start.1 = (bf16[16,512]{1,0:T(8,128)(2,1)}, bf16[16,512]{1,0:T(8,128)(2,1)S(1)}, u32[]{:S(2)}, u32[]{:S(2)}) collective-permute-start(bf16[16,512]{1,0:T(8,128)(2,1)} %param.12), channel_id=1, source_target_pairs={{0,256},{256,0},{1,257},{257,1},{2,258},{258,2},{3,259},{259,3},{4... | collective-permute-start | bytes 49160 | tf_op jit(solution)/shard_map/ppermute | solution.py:210
  17.2 7.1 %copy-start.4 = (bf16[16,512]{1,0:T(8,128)(2,1)S(1)}, bf16[16,512]{1,0:T(8,128)(2,1)}, u32[]{:S(2)}) copy-start(bf16[16,512]{1,0:T(8,128)(2,1)} %param.12) | copy-start | bytes 49156
  17.3 31.2 %copy-start.3 = (s32[1,8]{1,0:T(1,128)S(1)}, s32[1,8]{1,0:T(1,128)}, u32[]{:S(2)}) copy-start(s32[1,8]{1,0:T(1,128)} %len_ref) | copy-start | bytes 100
  24.4 10.6 %collective-permute-start.3 = (bf16[64,1024]{1,0:T(8,128)(2,1)S(1)}, bf16[64,1024]{1,0:T(8,128)(2,1)S(1)}, u32[]{:S(2)}, u32[]{:S(2)}) collective-permute-start(bf16[64,1024]{1,0:T(8,128)(2,1)S(1)} %convert_element_type.23), channel_id=1, source_target_pairs={{0,2},{2,0},{4,6},{6,4},{1,3},{3,1},{5,7},{7,5},{8,10},{10,8},{12,... | collective-permute-start | bytes 393224 | tf_op jit(solution)/shard_map/ppermute | solution.py:220
  27.5 11.5 %collective-permute-start.2 = (bf16[32,512]{1,0:T(8,128)(2,1)S(1)}, bf16[32,512]{1,0:T(8,128)(2,1)S(1)}, u32[]{:S(2)}, u32[]{:S(2)}) collective-permute-start(bf16[32,512]{1,0:T(8,128)(2,1)S(1)} %pad_maximum_fusion.2), channel_id=1, source_target_pairs={{0,128},{128,0},{1,129},{129,1},{2,130},{130,2},{3,131},{131,3},{4... | collective-permute-start | bytes 98312 | tf_op jit(solution)/shard_map/ppermute | solution.py:224
  35.0 11.0 %collective-permute-start.4 = (bf16[64,1024]{1,0:T(8,128)(2,1)S(1)}, bf16[64,1024]{1,0:T(8,128)(2,1)S(1)}, u32[]{:S(2)}, u32[]{:S(2)}) collective-permute-start(bf16[64,1024]{1,0:T(8,128)(2,1)S(1)} %fusion), channel_id=1, source_target_pairs={{0,4},{4,0},{2,6},{6,2},{1,5},{5,1},{3,7},{7,3},{8,12},{12,8},{10,... | collective-permute-start | bytes 393224 | tf_op jit(solution)/shard_map/ppermute | solution.py:221
  39.8 13.2 %all-to-all-start = ((bf16[4,64,512]{2,1,0:T(8,128)(2,1)}), bf16[4,64,512]{2,1,0:T(8,128)(2,1)S(1)}, u32[]{:S(2)}, u32[]{:S(2)}) async-start(bf16[4,64,512]{2,1,0:T(8,128)(2,1)} %broadcast_in_dim.2), calls=%async_computation | async-start | bytes 524288 | tf_op jit(solution)/shard_map/all_to_all | solution.py:198
  46.1 4.3 %collective-permute-start.5 = (bf16[64,1024]{1,0:T(8,128)(2,1)S(1)}, bf16[64,1024]{1,0:T(8,128)(2,1)S(1)}, u32[]{:S(2)}, u32[]{:S(2)}) collective-permute-start(bf16[64,1024]{1,0:T(8,128)(2,1)S(1)} %add_convert_fusion.o1_ref), channel_id=1, source_target_pairs={{0,1},{1,0},{2,3},{3,2},{4,5},{5,4},{6,7},{7,6},{8,9},{9,8},{10,11... | collective-permute-start | bytes 393224 | tf_op jit(solution)/shard_map/ppermute | solution.py:223
  52.9 7.1 %collective-permute-start.6 = (bf16[256,512]{1,0:T(8,128)(2,1)S(1)}, bf16[256,512]{1,0:T(8,128)(2,1)S(1)}, u32[]{:S(2)}, u32[]{:S(2)}) collective-permute-start(bf16[256,512]{1,0:T(8,128)(2,1)S(1)} %bitcast.7), channel_id=1, source_target_pairs={{0,32},{32,0},{1,33},{33,1},{2,34},{34,2},{3,35},{35,3},{4,36},{36... | collective-permute-start | bytes 786440 | tf_op jit(solution)/shard_map/ppermute | solution.py:227
  60.1 14.0 %collective-permute-start.7 = (bf16[512,512]{1,0:T(8,128)(2,1)S(1)}, bf16[512,512]{1,0:T(8,128)(2,1)S(1)}, u32[]{:S(2)}, u32[]{:S(2)}) collective-permute-start(bf16[512,512]{1,0:T(8,128)(2,1)S(1)} %pad_maximum_fusion.q1_ref), channel_id=1, source_target_pairs={{0,8},{8,0},{1,9},{9,1},{2,10},{10,2},{3,11},{11,3},{4,12},{12,4},... | collective-permute-start | bytes 1572872 | tf_op jit(solution)/shard_map/ppermute | solution.py:230

commit v5 on v4

--- a/solution.py
+++ b/solution.py
@@ -144,7 +144,7 @@
     )(scene, near(o1), near(o2), near(i))
 
 
-def score_kernel(f_ref, q1_ref, q2_ref, out_ref, own, turned, feat):
+def score_kernel(f_ref, q1_ref, q2_ref, q3_ref, q4_ref, out_ref, own, turned, feat):
     group = lax.axis_index("z") * 4 + lax.axis_index("y2") * 2
     total = f_ref[0].astype(f32)
     for t in range(1, 8):
@@ -166,7 +166,7 @@
             row = 0
             for axis in ORDER:
                 row = 2 * row + (bits[axis] > 0)
-            ref, row = (q1_ref, row) if row < 32 else (q2_ref, row - 32)
+            ref, row = (q1_ref, q2_ref, q3_ref, q4_ref)[row // 16], row % 16
             rows.append(ref[16 * row : 16 * row + 16, :])
         x = lax.dot_general(
             f, jnp.concatenate(rows, axis=0), (((1,), (1,)), ((), ())), preferred_element_type=f32
@@ -177,10 +177,10 @@
         out_ref[t ^ group] = x
 
 
-def partial_scores(f, q1, q2):
+def partial_scores(f, *q):
     return pl.pallas_call(
         score_kernel,
-        in_specs=[VMEM] * 3,
+        in_specs=[VMEM] * 5,
         out_specs=VMEM,
         out_shape=jax.ShapeDtypeStruct((8, 8, 128), f32),
         scratch_shapes=[
@@ -190,7 +190,7 @@
         ],
         compiler_params=pltpu.CompilerParams(vmem_limit_bytes=8 * 2**20),
         cost_estimate=pl.CostEstimate(flops=2 * 256 * 512 * 1024, bytes_accessed=2**20, transcendentals=0),
-    )(f, q1, q2)
+    )(f, *q)
 
 
 def gather(x, axes):
@@ -224,12 +224,13 @@
     q = jnp.concatenate([q, lax.ppermute(q, "y2", SWAP)], axis=0)
     q = gather(q, ("x1", "y1"))
     q, o1, o2 = tie((q, o1, o2))
-    q = jnp.concatenate([q, lax.ppermute(q, "y0", SWAP)], axis=0)
+    q_y = lax.ppermute(q, "y0", SWAP)
+    q_x = lax.ppermute(q, "x0", SWAP)
     f = features(scene, o1, o2, i)
-    q, f = tie((q, f))
-    q2 = lax.ppermute(q, "x0", SWAP)
+    q_y, q_x, f = tie((q_y, q_x, f))
+    q_xy = lax.ppermute(q_y, "x0", SWAP)
     f = lax.all_to_all(f, TENSOR, 0, 0)
-    scores = partial_scores(near(f), near(q), near(q2))
+    scores = partial_scores(near(f), near(q), near(q_y), near(q_x), near(q_xy))
     return jnp.sum(lax.all_to_all(scores, TENSOR, 0, 0), axis=0)
 
 

time: 86.3 us -> 85.9 us (level); the launches traced: 84.8 us -> 85.3 us
  starting transfers between devices: 39.8 us -> 42.1 us
  blocking collectives: 21.3 us -> 19.6 us
    ppermute x2 -> x3, starting transfers between devices: 4.17 us -> 6.42 us  [the longest x1 2.26 us: local(): q_x = lax.ppermute(q, 'x0', SWAP)]
    all_to_all x1, blocking collectives: 9.53 us -> 8.18 us  [local(): return jnp.sum(lax.all_to_all(scores, TENSOR, 0, 0), axis=0)]
    ppermute x2 -> x3, waiting for transfers between devices: 4.26 us -> 4.22 us  [the longest x1 2.22 us: local(): q_x = lax.ppermute(q, 'x0', SWAP)]
  transfers between devices with their start and end apart: 9 -> 10, of which waited for: 3 -> 4; matrix products, arithmetic and copies ran while one was open for 1% -> 1% of each run, Pallas kernels for 12% -> 12%
where the time goes in v5:
time: 85.9 us; the launch traced here: 85.3 us
  starting transfers between devices  42.1 us (49%)
  blocking collectives  19.6 us (23%)
  Pallas kernels  11 us (13%)
  waiting for transfers between devices  8.74 us (10%)
  local copies, waits for them, and re-layouts  1.88 us (2%)
  matrix products  1 us (1%)
    all_to_all x1, blocking collectives, local(): f = lax.all_to_all(f, TENSOR, 0, 0)  11.5 us
    ppermute x1, starting transfers between devices, local(): o = o1 + lax.ppermute(o2.astype(bf16), 'c', SWAP).astype(f32)  9.05 us
    all_to_all x1, blocking collectives, local(): return jnp.sum(lax.all_to_all(scores, TENSOR, 0, 0), axis=0)  8.18 us
    ppermute x1, starting transfers between devices, local(): q = jnp.concatenate([q, lax.ppermute(q, 'y2', SWAP)], axis=0)  7.46 us
    pallas_call x1, Pallas kernels, in_project(): pl.pallas_call(in_kernel, in_specs=[VMEM] * 3, out_specs=VMEM, out_shape=...  7.03 us
    ppermute x1, starting transfers between devices, local(): q = jnp.concatenate([queries, lax.ppermute(queries, 'z', SWAP)], axis=0)  5.4 us
    all_to_all x1, starting transfers between devices, gather(): lax.all_to_all(jnp.broadcast_to(x[None], (count,) + x.shape), axes, 0, 0)  4.25 us
    ppermute x1, starting transfers between devices, local(): o = o + lax.ppermute(o.astype(bf16), 'zl', FAR).astype(f32)  4 us
  transfers between devices with their start and end apart: 10, of which 4 were waited for; matrix products, arithmetic and copies ran while one was open for 1% of the time, Pallas kernels for 12%

profile of v5, /device:TPU:1, one launch (start us, length us, event | category | flops | bytes accessed | tf_op | source)
XLA Modules:
  0.0 85.3 jit_solution(1741015847403668584)
XLA Ops:
  0.0 0.0 copy-start
  0.0 1.1 %copy-done = bf16[2048,176]{0,1:T(8,128)(2,1)S(1)} copy-done((bf16[2048,176]{0,1:T(8,128)(2,1)S(1)}, bf16[2048,176]{0,1:T(8,128)(2,1)}, u32[]{:S(2)}) %copy-start) | copy-done | bytes 720920
  1.1 1.0 %fusion.1 = f32[64,2048]{1,0:T(8,128)S(1)} fusion(bf16[176,64]{0,1:T(8,128)(2,1)} %param.11, bf16[2048,176]{0,1:T(8,128)(2,1)S(1)} %copy-done), kind=kOutput, calls=%fused_computation.7 | convolution fusion | flops 46137344 | bytes 1267712 | tf_op jit(solution)/shard_map/dot_general | solution.py:211
  2.1 0.0 slice-start
  2.2 0.0 slice-start.1
  2.2 0.0 copy-start.1
  2.2 0.0 copy-start.2
  2.2 9.1 %collective-permute-start = (bf16[64,1024]{1,0:T(8,128)(2,1)S(1)}, bf16[64,1024]{1,0:T(8,128)(2,1)S(1)}, u32[]{:S(2)}, u32[]{:S(2)}) collective-permute-start(bf16[64,1024]{1,0:T(8,128)(2,1)S(1)} %dynamic-slice_convert_fusion), channel_id=1, source_target_pairs={{0,1},{1,0},{2,3},{3,2},{4,5},{5,4},{6,7},{7,6},{8,9},{9,8},{10,11... | collective-permute-start | bytes 393224 | tf_op jit(solution)/shard_map/ppermute | solution.py:215
  11.3 5.4 %collective-permute-start.1 = (bf16[16,512]{1,0:T(8,128)(2,1)}, bf16[16,512]{1,0:T(8,128)(2,1)S(1)}, u32[]{:S(2)}, u32[]{:S(2)}) collective-permute-start(bf16[16,512]{1,0:T(8,128)(2,1)} %param.12), channel_id=1, source_target_pairs={{0,256},{256,0},{1,257},{257,1},{2,258},{258,2},{3,259},{259,3},{4... | collective-permute-start | bytes 49160 | tf_op jit(solution)/shard_map/ppermute | solution.py:210
  16.7 0.5 shard_map.73.zero_ref
  17.2 0.0 slice-done
  17.2 0.0 slice-done.1
  17.2 0.0 copy-done.1
  17.2 0.0 copy-done.2
  17.2 0.0 copy-start.4
  17.3 0.0 copy-start.3
  17.3 7.0 %shard_map.74.i_ref = bf16[2,64,1024]{2,1,0:T(8,128)(2,1)S(1)} custom-call(bf16[2048,1408]{1,0:T(8,128)(2,1)S(1)} %bitcast.8, bf16[1408,768]{1,0:T(8,128)(2,1)S(1)} %copy-done.1, bf16[64,768]{1,0:T(8,128)(2,1)S(1)} %bitcast.9), custom_call_target="tpu_custom_call" | custom-call | flops 5234491392 | bytes 7929856 | tf_op jit(solution)/shard_map/pallas_call | solution.py:102
  24.3 0.0 collective-permute-done.1
  24.3 0.0 copy-done.4
  24.3 0.0 collective-permute-done
  24.4 3.1 %collective-permute-start.3 = (bf16[64,1024]{1,0:T(8,128)(2,1)S(1)}, bf16[64,1024]{1,0:T(8,128)(2,1)S(1)}, u32[]{:S(2)}, u32[]{:S(2)}) collective-permute-start(bf16[64,1024]{1,0:T(8,128)(2,1)S(1)} %convert_element_type.23), channel_id=1, source_target_pairs={{0,2},{2,0},{4,6},{6,4},{1,3},{3,1},{5,7},{7,5},{8,10},{10,8},{12,... | collective-permute-start | bytes 393224 | tf_op jit(solution)/shard_map/ppermute | solution.py:220
  27.5 7.5 %collective-permute-start.2 = (bf16[32,512]{1,0:T(8,128)(2,1)S(1)}, bf16[32,512]{1,0:T(8,128)(2,1)S(1)}, u32[]{:S(2)}, u32[]{:S(2)}) collective-permute-start(bf16[32,512]{1,0:T(8,128)(2,1)S(1)} %pad_maximum_fusion.1), channel_id=1, source_target_pairs={{0,128},{128,0},{1,129},{129,1},{2,130},{130,2},{3,131},{131,3},{4... | collective-permute-start | bytes 98312 | tf_op jit(solution)/shard_map/ppermute | solution.py:224
  35.0 0.0 collective-permute-done.3
  35.0 4.0 %collective-permute-start.4 = (bf16[64,1024]{1,0:T(8,128)(2,1)S(1)}, bf16[64,1024]{1,0:T(8,128)(2,1)S(1)}, u32[]{:S(2)}, u32[]{:S(2)}) collective-permute-start(bf16[64,1024]{1,0:T(8,128)(2,1)S(1)} %fusion), channel_id=1, source_target_pairs={{0,4},{4,0},{2,6},{6,2},{1,5},{5,1},{3,7},{7,3},{8,12},{12,8},{10,... | collective-permute-start | bytes 393224 | tf_op jit(solution)/shard_map/ppermute | solution.py:221
  39.0 0.0 collective-permute-done.2
  39.1 0.7 broadcast_in_dim.2
  39.8 4.3 %all-to-all-start = ((bf16[4,64,512]{2,1,0:T(8,128)(2,1)}), bf16[4,64,512]{2,1,0:T(8,128)(2,1)S(1)}, u32[]{:S(2)}, u32[]{:S(2)}) async-start(bf16[4,64,512]{2,1,0:T(8,128)(2,1)} %broadcast_in_dim.2), calls=%async_computation | async-start | bytes 524288 | tf_op jit(solution)/shard_map/all_to_all | solution.py:198
  44.0 2.0 %collective-permute-done.4 = bf16[64,1024]{1,0:T(8,128)(2,1)S(1)} collective-permute-done((bf16[64,1024]{1,0:T(8,128)(2,1)S(1)}, bf16[64,1024]{1,0:T(8,128)(2,1)S(1)}, u32[]{:S(2)}, u32[]{:S(2)}) %collective-permute-start.4) | collective-permute-done | bytes 131104 | tf_op jit(solution)/shard_map/ppermute | solution.py:221
  46.1 2.4 %collective-permute-start.5 = (bf16[64,1024]{1,0:T(8,128)(2,1)S(1)}, bf16[64,1024]{1,0:T(8,128)(2,1)S(1)}, u32[]{:S(2)}, u32[]{:S(2)}) collective-permute-start(bf16[64,1024]{1,0:T(8,128)(2,1)S(1)} %add_convert_fusion.o1_ref), channel_id=1, source_target_pairs={{0,1},{1,0},{2,3},{3,2},{4,5},{5,4},{6,7},{7,6},{8,9},{9,8},{10,11... | collective-permute-start | bytes 393224 | tf_op jit(solution)/shard_map/ppermute | solution.py:223
  48.5 0.0 copy-done.3
  48.5 1.9 %shard_map.75.scene_ref = s32[16]{0:T(128)S(1)} custom-call(s32[1]{0:T(128)} %shard_map.73.zero_ref, s32[1,8]{1,0:T(1,128)S(1)} %copy-done.3), custom_call_target="tpu_custom_call" | custom-call | flops 1000000 | bytes 64 | tf_op jit(solution)/shard_map/pallas_call | solution.py:59
  50.4 0.0 collective-permute-done.5.o2_ref
  50.4 2.5 %all-to-all-done = bf16[4,64,512]{2,1,0:T(8,128)(2,1)S(1)} async-done(((bf16[4,64,512]{2,1,0:T(8,128)(2,1)}), bf16[4,64,512]{2,1,0:T(8,128)(2,1)S(1)}, u32[]{:S(2)}, u32[]{:S(2)}) %all-to-all-start) | async-done | bytes 262176 | tf_op jit(solution)/shard_map/all_to_all | solution.py:198
  52.9 1.9 %collective-permute-start.6 = (bf16[256,512]{1,0:T(8,128)(2,1)S(1)}, bf16[256,512]{1,0:T(8,128)(2,1)S(1)}, u32[]{:S(2)}, u32[]{:S(2)}) collective-permute-start(bf16[256,512]{1,0:T(8,128)(2,1)S(1)} %bitcast.4), channel_id=1, source_target_pairs={{0,32},{32,0},{1,33},{33,1},{2,34},{34,2},{3,35},{35,3},{4,36},{36... | collective-permute-start | bytes 786440 | tf_op jit(solution)/shard_map/ppermute | solution.py:227
  54.8 2.3 %collective-permute-start.7 = (bf16[256,512]{1,0:T(8,128)(2,1)S(1)}, bf16[256,512]{1,0:T(8,128)(2,1)S(1)}, u32[]{:S(2)}, u32[]{:S(2)}) collective-permute-start(bf16[256,512]{1,0:T(8,128)(2,1)S(1)} %bitcast.5), channel_id=1, source_target_pairs={{0,8},{8,0},{1,9},{9,1},{2,10},{10,2},{3,11},{11,3},{4,12},{12,4},... | collective-permute-start | bytes 786440 | tf_op jit(solution)/shard_map/ppermute | solution.py:228
  57.1 0.9 %shard_map.76 = bf16[8,32,128]{2,1,0:T(8,128)(2,1)S(1)} custom-call(s32[16]{0:T(128)S(1)} %shard_map.75.scene_ref, bf16[64,1024]{1,0:T(8,128)(2,1)S(1)} %add_convert_fusion.o1_ref, bf16[64,1024]{1,0:T(8,128)(2,1)S(1)} %collective-permute-done.5.o2_ref, bf16[2,64,1024]{2,1,0:T(8,128)(2,1)S(1)} %shard_map.74.i_ref), custom_call_target="tpu_custom_call" | custom-call | flops 20000000000 | bytes 1048576 | tf_op jit(solution)/shard_map/pallas_call | solution.py:136
  58.0 2.0 %collective-permute-done.6.q2_ref = bf16[256,512]{1,0:T(8,128)(2,1)S(1)} collective-permute-done((bf16[256,512]{1,0:T(8,128)(2,1)S(1)}, bf16[256,512]{1,0:T(8,128)(2,1)S(1)}, u32[]{:S(2)}, u32[]{:S(2)}) %collective-permute-start.6) | collective-permute-done | bytes 262176 | tf_op jit(solution)/shard_map/ppermute | solution.py:227
  60.0 2.2 %collective-permute-done.7.q3_ref = bf16[256,512]{1,0:T(8,128)(2,1)S(1)} collective-permute-done((bf16[256,512]{1,0:T(8,128)(2,1)S(1)}, bf16[256,512]{1,0:T(8,128)(2,1)S(1)}, u32[]{:S(2)}, u32[]{:S(2)}) %collective-permute-start.7) | collective-permute-done | bytes 262176 | tf_op jit(solution)/shard_map/ppermute | solution.py:228
  62.3 2.2 %collective-permute-start.8 = (bf16[256,512]{1,0:T(8,128)(2,1)S(1)}, bf16[256,512]{1,0:T(8,128)(2,1)S(1)}, u32[]{:S(2)}, u32[]{:S(2)}) collective-permute-start(bf16[256,512]{1,0:T(8,128)(2,1)S(1)} %collective-permute-done.6.q2_ref), channel_id=1, source_target_pairs={{0,8},{8,0},{1,9},{9,1},{2,10},{10,2},{3,11},{11,3},{4,12},{12,4},... | collective-permute-start | bytes 786440 | tf_op jit(solution)/shard_map/ppermute | solution.py:231
  64.5 11.5 %all_to_all.15.f_ref = bf16[8,32,128]{2,1,0:T(8,128)(2,1)S(1)} all-to-all(bf16[8,32,128]{2,1,0:T(8,128)(2,1)S(1)} %shard_map.76), channel_id=1, replica_groups=mesh['z'=2,'y2'=2,'y1'=2,'y0'=2,'x1'=2,'x0'=2,'zl'=4,'c'=2] {'zl','c'}, dimensions={0} | all-to-all | bytes 131072 | tf_op jit(solution)/shard_map/all_to_all | solution.py:232
  76.0 0.0 collective-permute-done.8.q4_ref
  76.0 0.6 shard_map.77
  76.6 8.2 %all_to_all.16 = f32[8,8,128]{2,1,0:T(8,128)S(1)} all-to-all(f32[8,8,128]{2,1,0:T(8,128)S(1)} %shard_map.77), channel_id=1, replica_groups=mesh['z'=2,'y2'=2,'y1'=2,'y0'=2,'x1'=2,'x0'=2,'zl'=4,'c'=2] {'zl','c'}, dimensions={0} | all-to-all | bytes 65536 | tf_op jit(solution)/shard_map/all_to_all | solution.py:234
  84.7 0.6 reduce_sum.9
  (8 shorter events, 0.2 us)
Async XLA Ops:
  0.0 1.1 %copy-start = (bf16[2048,176]{0,1:T(8,128)(2,1)S(1)}, bf16[2048,176]{0,1:T(8,128)(2,1)}, u32[]{:S(2)}) copy-start(bf16[2048,176]{0,1:T(8,128)(2,1)} %param.9) | copy-start | bytes 2162692
  2.1 15.1 %slice-start = ((s8[5767168]{0:T(1024)(128)(4,1)}), s8[4194304]{0:T(1024)(128)(4,1)S(1)}, s32[]{:S(2)}) async-start(s8[5767168]{0:T(1024)(128)(4,1)} %bitcast.7), calls=%async_computation.3 | async-start | bytes 8388608
  2.2 15.0 %slice-start.1 = ((s8[5767168]{0:T(1024)(128)(4,1)}), s8[1572864]{0:T(1024)(128)(4,1)S(1)}, s32[]{:S(2)}) async-start(s8[5767168]{0:T(1024)(128)(4,1)} %bitcast.7), calls=%async_computation.4 | async-start | bytes 3145728
  2.2 15.0 %copy-start.1 = (bf16[1408,768]{1,0:T(8,128)(2,1)S(1)}, bf16[1408,768]{1,0:T(8,128)(2,1)}, u32[]{:S(2)}) copy-start(bf16[1408,768]{1,0:T(8,128)(2,1)} %w_ref.1) | copy-start | bytes 6488068
  2.2 15.0 %copy-start.2 = (bf16[768,64]{0,1:T(8,128)(2,1)S(1)}, bf16[768,64]{0,1:T(8,128)(2,1)}, u32[]{:S(2)}) copy-start(bf16[768,64]{0,1:T(8,128)(2,1)} %param.10) | copy-start | bytes 294916
  2.2 22.1 %collective-permute-start = (bf16[64,1024]{1,0:T(8,128)(2,1)S(1)}, bf16[64,1024]{1,0:T(8,128)(2,1)S(1)}, u32[]{:S(2)}, u32[]{:S(2)}) collective-permute-start(bf16[64,1024]{1,0:T(8,128)(2,1)S(1)} %dynamic-slice_convert_fusion), channel_id=1, source_target_pairs={{0,1},{1,0},{2,3},{3,2},{4,5},{5,4},{6,7},{7,6},{8,9},{9,8},{10,11... | collective-permute-start | bytes 393224 | tf_op jit(solution)/shard_map/ppermute | solution.py:215
  11.3 13.0 %collective-permute-start.1 = (bf16[16,512]{1,0:T(8,128)(2,1)}, bf16[16,512]{1,0:T(8,128)(2,1)S(1)}, u32[]{:S(2)}, u32[]{:S(2)}) collective-permute-start(bf16[16,512]{1,0:T(8,128)(2,1)} %param.12), channel_id=1, source_target_pairs={{0,256},{256,0},{1,257},{257,1},{2,258},{258,2},{3,259},{259,3},{4... | collective-permute-start | bytes 49160 | tf_op jit(solution)/shard_map/ppermute | solution.py:210
  17.2 7.1 %copy-start.4 = (bf16[16,512]{1,0:T(8,128)(2,1)S(1)}, bf16[16,512]{1,0:T(8,128)(2,1)}, u32[]{:S(2)}) copy-start(bf16[16,512]{1,0:T(8,128)(2,1)} %param.12) | copy-start | bytes 49156
  17.3 31.2 %copy-start.3 = (s32[1,8]{1,0:T(1,128)S(1)}, s32[1,8]{1,0:T(1,128)}, u32[]{:S(2)}) copy-start(s32[1,8]{1,0:T(1,128)} %len_ref) | copy-start | bytes 100
  24.4 10.6 %collective-permute-start.3 = (bf16[64,1024]{1,0:T(8,128)(2,1)S(1)}, bf16[64,1024]{1,0:T(8,128)(2,1)S(1)}, u32[]{:S(2)}, u32[]{:S(2)}) collective-permute-start(bf16[64,1024]{1,0:T(8,128)(2,1)S(1)} %convert_element_type.23), channel_id=1, source_target_pairs={{0,2},{2,0},{4,6},{6,4},{1,3},{3,1},{5,7},{7,5},{8,10},{10,8},{12,... | collective-permute-start | bytes 393224 | tf_op jit(solution)/shard_map/ppermute | solution.py:220
  27.5 11.5 %collective-permute-start.2 = (bf16[32,512]{1,0:T(8,128)(2,1)S(1)}, bf16[32,512]{1,0:T(8,128)(2,1)S(1)}, u32[]{:S(2)}, u32[]{:S(2)}) collective-permute-start(bf16[32,512]{1,0:T(8,128)(2,1)S(1)} %pad_maximum_fusion.1), channel_id=1, source_target_pairs={{0,128},{128,0},{1,129},{129,1},{2,130},{130,2},{3,131},{131,3},{4... | collective-permute-start | bytes 98312 | tf_op jit(solution)/shard_map/ppermute | solution.py:224
  35.0 11.0 %collective-permute-start.4 = (bf16[64,1024]{1,0:T(8,128)(2,1)S(1)}, bf16[64,1024]{1,0:T(8,128)(2,1)S(1)}, u32[]{:S(2)}, u32[]{:S(2)}) collective-permute-start(bf16[64,1024]{1,0:T(8,128)(2,1)S(1)} %fusion), channel_id=1, source_target_pairs={{0,4},{4,0},{2,6},{6,2},{1,5},{5,1},{3,7},{7,3},{8,12},{12,8},{10,... | collective-permute-start | bytes 393224 | tf_op jit(solution)/shard_map/ppermute | solution.py:221
  39.8 13.2 %all-to-all-start = ((bf16[4,64,512]{2,1,0:T(8,128)(2,1)}), bf16[4,64,512]{2,1,0:T(8,128)(2,1)S(1)}, u32[]{:S(2)}, u32[]{:S(2)}) async-start(bf16[4,64,512]{2,1,0:T(8,128)(2,1)} %broadcast_in_dim.2), calls=%async_computation | async-start | bytes 524288 | tf_op jit(solution)/shard_map/all_to_all | solution.py:198
  46.1 4.3 %collective-permute-start.5 = (bf16[64,1024]{1,0:T(8,128)(2,1)S(1)}, bf16[64,1024]{1,0:T(8,128)(2,1)S(1)}, u32[]{:S(2)}, u32[]{:S(2)}) collective-permute-start(bf16[64,1024]{1,0:T(8,128)(2,1)S(1)} %add_convert_fusion.o1_ref), channel_id=1, source_target_pairs={{0,1},{1,0},{2,3},{3,2},{4,5},{5,4},{6,7},{7,6},{8,9},{9,8},{10,11... | collective-permute-start | bytes 393224 | tf_op jit(solution)/shard_map/ppermute | solution.py:223
  52.9 7.1 %collective-permute-start.6 = (bf16[256,512]{1,0:T(8,128)(2,1)S(1)}, bf16[256,512]{1,0:T(8,128)(2,1)S(1)}, u32[]{:S(2)}, u32[]{:S(2)}) collective-permute-start(bf16[256,512]{1,0:T(8,128)(2,1)S(1)} %bitcast.4), channel_id=1, source_target_pairs={{0,32},{32,0},{1,33},{33,1},{2,34},{34,2},{3,35},{35,3},{4,36},{36... | collective-permute-start | bytes 786440 | tf_op jit(solution)/shard_map/ppermute | solution.py:227
  54.8 7.4 %collective-permute-start.7 = (bf16[256,512]{1,0:T(8,128)(2,1)S(1)}, bf16[256,512]{1,0:T(8,128)(2,1)S(1)}, u32[]{:S(2)}, u32[]{:S(2)}) collective-permute-start(bf16[256,512]{1,0:T(8,128)(2,1)S(1)} %bitcast.5), channel_id=1, source_target_pairs={{0,8},{8,0},{1,9},{9,1},{2,10},{10,2},{3,11},{11,3},{4,12},{12,4},... | collective-permute-start | bytes 786440 | tf_op jit(solution)/shard_map/ppermute | solution.py:228
  62.3 13.7 %collective-permute-start.8 = (bf16[256,512]{1,0:T(8,128)(2,1)S(1)}, bf16[256,512]{1,0:T(8,128)(2,1)S(1)}, u32[]{:S(2)}, u32[]{:S(2)}) collective-permute-start(bf16[256,512]{1,0:T(8,128)(2,1)S(1)} %collective-permute-done.6.q2_ref), channel_id=1, source_target_pairs={{0,8},{8,0},{1,9},{9,1},{2,10},{10,2},{3,11},{11,3},{4,12},{12,4},... | collective-permute-start | bytes 786440 | tf_op jit(solution)/shard_map/ppermute | solution.py:231
